TPU v7x, 128 devices: a whole 4x4x4 slice. The times are simulated.
128 devices in a mesh: dp: 4 (over y_lo, core), basis: 32 (over z, y_hi, x).
Axes of the slice: x: 4, y: 4 (y_hi: 2, y_lo: 2; y = y_hi * 2 + y_lo), z: 4, core: 2. Of those that a mesh axis runs over, the one named last changes fastest.
Arguments:
- train_act: bfloat16 [1024, 18944], P('dp', 'basis'), may hold values from -6 to 6
- train_out_grad: bfloat16 [1024, 3584], P('dp', 'basis'), may hold values from -6 to 6
- query_act: bfloat16 [256, 18944], P('dp', 'basis'), may hold values from -6 to 6
- query_out_grad: bfloat16 [256, 3584], P('dp', 'basis'), may hold values from -6 to 6
- in_basis: bfloat16 [18944, 18944], P('dp', 'basis'), may hold values from -0.046875 to 0.046875
- out_basis: bfloat16 [3584, 3584], P('basis'), may hold values from -0.09375 to 0.09375
- eigvals: bfloat16 [3584, 18944], P(None, 'basis'), may hold values from 0.5 to 8
- pair_ids: int32 [256], replicated, may hold values from 0 to 3
- seq_lengths: int32 [4, 4], P('dp'), may hold values from 1 to 128, 256 in all within a row
Outputs:
- scores: float32 [4, 16], P(None, 'dp')
Inputs may be any that keep to these rules, and one draw needn't show every extreme that they name: `seq_lengths`: each row sums to 256, and its largest entry is 128.
All inputs are finite; a program needn't handle non-finite values.
Results may differ from a plain program's by a relative error of at most 0.0075.
Values may be sent and summed in bfloat16 or wider, within the bound.
A program may use at most 192 MiB of HBM per device.

v0:
```python
import math

import jax
import jax.numpy as jnp
from jax import lax
from jax.sharding import PartitionSpec as P

D = 3584
FF = 18944
PAIRS = 4
SEQ_DP = 4
TOK_DP = 256
QTOK_DP = 64


DAMPING = 0.5


def on_device(
    train_act,
    train_out_grad,
    query_act,
    query_out_grad,
    in_basis,
    out_basis,
    eigvals,
    pair_ids,
    seq_lengths,
):
    tok_rows = train_act.shape[0]
    act_rows = jnp.concatenate([train_act, query_act], axis=0)
    grad_rows = jnp.concatenate([train_out_grad, query_out_grad], axis=0)
    full_act = lax.all_gather(act_rows, "basis", axis=1, tiled=True)
    rotated = jnp.dot(
        full_act,
        lax.all_gather(in_basis, "dp", axis=0, tiled=True),
        preferred_element_type=jnp.float32,
    )
    rot_act = rotated.astype(jnp.bfloat16)
    contract = (((0,), (1,)), ((), ()))
    grad_term = lax.dot_general(out_basis, grad_rows, contract, preferred_element_type=jnp.float32)
    rot_grad = lax.psum(grad_term, "basis").astype(jnp.bfloat16)
    query_rot_act, query_rot_grad = (
        lax.all_gather(rot_act[tok_rows:], "dp", axis=0, tiled=True),
        lax.all_gather(rot_grad[:, tok_rows:], "dp", axis=1, tiled=True),
    )
    hot_table = (pair_ids[None, :] == jnp.arange(PAIRS, dtype=jnp.int32)[:, None]).astype(
        jnp.bfloat16
    )
    masked = query_rot_grad[None, :, :] * hot_table[:, None, :]
    query_rot = jnp.einsum("pdq,qj->pdj", masked, query_rot_act, preferred_element_type=jnp.float32)
    precond = (query_rot / (eigvals.astype(jnp.float32) + DAMPING)).astype(jnp.bfloat16)
    projected = jnp.einsum(
        "pdj,tj->pdt", precond, rot_act[:tok_rows], preferred_element_type=jnp.float32
    )
    token_score = jnp.sum(
        projected * rot_grad[:, :tok_rows].astype(jnp.float32)[None, :, :], axis=1
    )
    lengths = seq_lengths[0]
    seq_ends = jnp.cumsum(lengths)
    seq_starts = seq_ends - lengths
    positions = jnp.arange(tok_rows, dtype=jnp.int32)
    member = (
        (positions[None, :] >= seq_starts[:, None]) & (positions[None, :] < seq_ends[:, None])
    ).astype(jnp.float32)
    partial_scores = jnp.dot(token_score, member.T, preferred_element_type=jnp.float32)
    score_scale = SEQ_DP / math.sqrt(D * FF * TOK_DP * QTOK_DP)
    return lax.psum(partial_scores, "basis") * score_scale


def solution(mesh):
    in_specs = (
        P("dp", "basis"),
        P("dp", "basis"),
        P("dp", "basis"),
        P("dp", "basis"),
        P("dp", "basis"),
        P("basis", None),
        P(None, "basis"),
        P(),
        P("dp", None),
    )
    out_specs = P(None, "dp")
    return jax.shard_map(
        on_device, mesh=mesh, in_specs=in_specs, out_specs=out_specs, check_vma=False
    )
```

profile of v0, /device:TPU:0, one launch (start us, length us, event | category | flops | bytes accessed | tf_op | source)
XLA Modules:
  0.0 726.1 jit_solution(2292086755339644883)
XLA Ops:
  6.5 0.0 copy-start
  6.5 0.0 copy-start.2
  6.5 0.0 all-gather.5.cloned.1.call-start
  6.5 0.9 copy.20
  7.5 0.2 copy-done
  7.7 0.0 copy-start.3
  7.7 3.7 convolution_bitcast_fusion
  11.4 216.9 %all-reduce.1 = bf16[3584,320]{0,1:T(8,128)(2,1)S(1)} all-reduce(f32[3584,320]{0,1:T(8,128)} %convolution_bitcast_fusion), channel_id=1, replica_groups=mesh['dp'=4,'basis'=32] {'basis'}, use_global_device_ids=true, to_apply=%region_0.0 | all-reduce | flops 1146880 | bytes 6881280 | tf_op jit(solution)/shard_map/psum | solution.py:42
  228.3 0.8 slice.16
  229.1 0.0 all-gather.5.cloned.1.call-update
  229.1 0.0 all-gather.9.cloned.1.call-start
  229.2 0.0 copy-done.2
  229.2 0.2 copy.22
  229.4 0.0 copy-done.3
  229.4 0.8 maximum_bitcast_fusion
  230.2 0.0 all-gather.9.cloned.1.call-update
  230.2 0.0 copy-start.5
  230.2 0.0 copy-start.4
  230.3 0.0 all-gather.7.cloned.1.call-start
  230.3 0.7 all-gather.7.cloned.1.call-update
  231.0 2.3 slice_convert_fusion
  233.3 5.2 copy.25
  238.5 0.0 copy-done.5
  238.5 0.2 reduce-window.7
  238.7 0.0 copy-done.4
  238.7 6.6 convert_add_fusion
  245.3 5.5 all-gather.5.cloned.1.call-done
  250.8 2.9 copy.21
  253.7 133.8 %all-gather.9.cloned.1.call-done = bf16[32,592,320]{1,2,0:T(8,128)(2,1)} async-done(((bf16[1,592,320]{1,2,0:T(8,128)(2,1)}), bf16[32,592,320]{1,2,0:T(8,128)(2,1)}) %all-gather.9.cloned.1.call-update) | async-done | bytes 12124176 | tf_op jit(solution)/shard_map/all_gather | solution.py:33
  387.5 16.8 %copy.23 = bf16[32,592,320]{1,0,2:T(8,128)(2,1)} copy(bf16[32,592,320]{1,2,0:T(8,128)(2,1)} %all-gather.9.cloned.1.call-done) | data formatting | bytes 24248320 | tf_op jit(solution)/shard_map/all_gather | solution.py:33
  404.3 26.2 %reshape.52 = bf16[18944,320]{0,1:T(8,128)(2,1)} reshape(bf16[32,592,320]{1,0,2:T(8,128)(2,1)} %copy.23) | data formatting | bytes 24248320
  430.5 155.5 %all-gather.7.cloned.1.call-done = bf16[18944,592]{0,1:T(8,128)(2,1)} async-done(((bf16[4736,592]{0,1:T(8,128)(2,1)}), bf16[18944,592]{0,1:T(8,128)(2,1)}) %all-gather.7.cloned.1.call-update) | async-done | bytes 22429712 | tf_op jit(solution)/shard_map/all_gather | solution.py:36
  586.1 15.8 %convolution_convert_fusion = bf16[320,592]{1,0:T(8,128)(2,1)S(1)} fusion(bf16[18944,320]{0,1:T(8,128)(2,1)} %reshape.52, bf16[18944,592]{0,1:T(8,128)(2,1)} %all-gather.7.cloned.1.call-done), kind=kOutput, calls=%fused_computation.10 | convolution fusion | flops 7177692160 | bytes 34932736 | tf_op jit(solution)/shard_map/dot_general | solution.py:34
  601.9 7.0 all_gather.15
  608.9 0.0 copy-start.1
  608.9 13.9 %multiply_reduce_fusion = bf16[4,256]{1,0:T(4,128)(2,1)S(1)} fusion(f32[3584,592]{0,1:T(8,128)} %convert_add_fusion, f32[3584,256]{1,0:T(8,128)} %copy.25, bf16[4,256]{1,0:T(4,128)(2,1)S(1)} %fusion.14, bf16[3584,256]{1,0:T(8,128)(2,1)S(1)} %copy.21, bf16[320,592]{1,0:T(8,128)(2,1)S(1)} %convolution_convert_fusion, bf16[256,592]{1,0:T(8,128)(2,1)S(1)} %all_gather.15), kind=kOutput, calls=%fused_computation.2 | convolution fusion | flops 8718580736 | bytes 14651392 | tf_op jit(solution)/shard_map/pdj,tj->pdt/dot_general | solution.py:53
  622.7 0.2 fusion.16
  622.9 96.1 %psum.15 = f32[4,4]{1,0:T(4,128)S(1)} all-reduce(f32[4,4]{1,0:T(4,128)S(1)} %fusion.16), channel_id=1, replica_groups=mesh['dp'=4,'basis'=32] {'basis'}, use_global_device_ids=true, to_apply=%region_3.4 | all-reduce | flops 16 | bytes 128 | tf_op jit(solution)/shard_map/psum | solution.py:68
  719.0 0.6 broadcast_multiply_fusion
  719.6 0.0 copy-done.1
  (3 shorter events, 0.0 us)
Async XLA Ops:
  6.5 1.2 copy-start
  6.5 222.7 %copy-start.2 = (bf16[256,592]{0,1:T(8,128)(2,1)S(1)}, bf16[256,592]{0,1:T(8,128)(2,1)}, u32[]{:S(2)}) copy-start(bf16[256,592]{0,1:T(8,128)(2,1)} %param.9) | copy-start | bytes 909316
  6.5 244.3 %all-gather.5.cloned.1.call-start = ((), (), s32[]{:S(2)}) async-start(), calls=%async_computation | async-start | bytes 2293760 | tf_op jit(solution)/shard_map/all_gather | solution.py:45
  7.7 221.7 %copy-start.3 = (bf16[64,592]{1,0:T(8,128)(2,1)S(1)}, bf16[64,592]{1,0:T(8,128)(2,1)}, u32[]{:S(2)}) copy-start(bf16[64,592]{1,0:T(8,128)(2,1)} %param.11) | copy-start | bytes 227332
  229.1 158.4 %all-gather.9.cloned.1.call-start = ((), (), s32[]{:S(2)}) async-start(), calls=%async_computation.2 | async-start | bytes 13516800 | tf_op jit(solution)/shard_map/all_gather | solution.py:33
  230.2 8.3 %copy-start.5 = (s32[1,4]{1,0:T(1,128)S(1)}, s32[1,4]{1,0:T(1,128)}, u32[]{:S(2)}) copy-start(s32[1,4]{1,0:T(1,128)} %param.17) | copy-start | bytes 52
  230.2 8.4 %copy-start.4 = (s32[256]{0:T(256)S(1)}, s32[256]{0:T(256)}, u32[]{:S(2)}) copy-start(s32[256]{0:T(256)} %param.16) | copy-start | bytes 3076
  230.3 355.8 %all-gather.7.cloned.1.call-start = ((), (), s32[]{:S(2)}) async-start(), calls=%async_computation.1 | async-start | bytes 28037120 | tf_op jit(solution)/shard_map/all_gather | solution.py:36
  608.9 110.7 %copy-start.1 = (bf16[112,3584]{1,0:T(8,128)(2,1)S(1)}, bf16[112,3584]{1,0:T(8,128)(2,1)}, u32[]{:S(2)}) copy-start(bf16[112,3584]{1,0:T(8,128)(2,1)} %param.14) | copy-start | bytes 2408452
Sparse Core Ops, SparseCore 0:
  229.3 21.5 all-gather.4
  253.9 133.5 all-gather.8
  389.2 196.7 all-gather.6
where the time goes:
time: 727 us; the launch traced here: 726 us
  blocking collectives  320 us (44%)
  waiting for transfers between devices  296 us (41%)
  local copies, waits for them, and re-layouts  53.3 us (7%)
  matrix products  33.5 us (5%)
  between operations  13.2 us (2%)
  other arithmetic  10.5 us (1%)
    psum x1, blocking collectives, on_device(): rot_grad = lax.psum(grad_term, 'basis').astype(jnp.bfloat16)  217 us
    all_gather x1, waiting for transfers between devices, on_device(): lax.all_gather(in_basis, 'dp', axis=0, tiled=True)  156 us
    all_gather x1, waiting for transfers between devices, on_device(): full_act = lax.all_gather(act_rows, 'basis', axis=1, tiled=True)  134 us
    psum x1, blocking collectives, on_device(): return lax.psum(partial_scores, 'basis') * score_scale  96.1 us
    unnamed x15, local copies, waits for them, and re-layouts  27.6 us
    all_gather x1, local copies, waits for them, and re-layouts, on_device(): full_act = lax.all_gather(act_rows, 'basis', axis=1, tiled=True)  16.8 us
    dot_general x1, matrix products, on_device(): jnp.dot(full_act, lax.all_gather(in_basis, 'dp', axis=0, tiled=True), pre...  15.8 us
  transfers between devices with their start and end apart: 3, of which 3 were waited for; matrix products, arithmetic and copies ran while one was open for 8% of the time, Pallas kernels for 0%

commit v1 on v0

--- a/solution.py
+++ b/solution.py
@@ -1,8 +1,11 @@
+import functools
 import math
 
 import jax
 import jax.numpy as jnp
 from jax import lax
+from jax.experimental import pallas as pl
+from jax.experimental.pallas import tpu as pltpu
 from jax.sharding import PartitionSpec as P
 
 D = 3584
@@ -11,9 +14,293 @@
 SEQ_DP = 4
 TOK_DP = 256
 QTOK_DP = 64
-
+ROWS = TOK_DP + QTOK_DP
+COLS = FF // 32
 
 DAMPING = 0.5
+MESH = pl.DeviceIdType.MESH
+
+UNIT = 2 * ROWS
+RB = 384
+
+
+def place():
+    dp, b = lax.axis_index("dp"), lax.axis_index("basis")
+    x, y, z, c = b % 4, ((b // 4) % 2) * 2 + dp // 2, b // 8, dp % 2
+    return x, y, z, c
+
+
+def device(x, y, z, c):
+    x, y, z = (x + 4) % 4, (y + 4) % 4, (z + 4) % 4
+    return ((y % 2) * 2 + c, z * 8 + (y // 2) * 4 + x)
+
+
+def turn(i):
+    return jnp.where(i == 2, 3, jnp.where(i == 3, 2, i))
+
+
+def rotate_kernel(act, w_hbm, out, units, other, w, w_sem, own_sem, s0, r0, rb, ra, rob, roa, szb, syb, sxb, sxa, sya, sya2, sza):
+    x, y, z, c = place()
+    d = 2 * (y % 2) + c
+    zeta = (z - d + 4) % 4
+    sign = 1 - 2 * c
+    pi = (sign * zeta + 4) % 4
+    is_own, is_other = zeta == 0, zeta == 2
+
+    def slot(xs, ys):
+        return ((xs + 4) % 4) * 4 + (ys + 4) % 4
+
+    here = slot(x, y)
+    beta, alpha = pl.ds(0, RB), pl.ds(RB, UNIT - RB)
+
+    def copy(src, dst, send, recv, target):
+        return pltpu.make_async_remote_copy(
+            src_ref=src, dst_ref=dst, send_sem=send, recv_sem=recv, device_id=target, device_id_type=MESH
+        )
+
+    partners = [device(x + o, y, z, c) for o in (1, 2, 3)]
+    partners += [device(x, y + o, z, c) for o in (1, 2, 3)]
+    partners += [device(x, y, z + o, c) for o in (1, 2, 3)]
+    partners += [device(x, y, z, 1 - c)]
+    core = partners[-1]
+
+    w_copy = pltpu.make_async_copy(w_hbm, w, w_sem)
+    w_copy.start()
+    barrier = pltpu.get_barrier_semaphore()
+    for p in partners:
+        pl.semaphore_signal(barrier, inc=1, device_id=p, device_id_type=MESH)
+    pl.semaphore_wait(barrier, len(partners))
+
+    mine = pl.ds(pl.multiple_of(c * ROWS, ROWS), ROWS)
+    theirs = pl.ds(pl.multiple_of((1 - c) * ROWS, ROWS), ROWS)
+    partner_zeta = (zeta - sign + 4) % 4
+    to_units = copy(act, units.at[here, mine], s0, r0, core)
+    to_other = copy(act, other.at[x, mine], s0, r0, core)
+
+    @pl.when(partner_zeta == 0)
+    def _():
+        to_units.start()
+
+    @pl.when(partner_zeta == 2)
+    def _():
+        to_other.start()
+
+    own_units = pltpu.make_async_copy(act, units.at[here, mine], own_sem)
+    own_other = pltpu.make_async_copy(act, other.at[x, mine], own_sem)
+
+    @pl.when(is_own)
+    def _():
+        own_units.start()
+        own_units.wait()
+        copy(act, units.at[here, theirs], s0, r0, core).wait_recv()
+
+    @pl.when(is_other)
+    def _():
+        own_other.start()
+        own_other.wait()
+        copy(act, other.at[x, theirs], s0, r0, core).wait_recv()
+
+    def z_beta(i, from_units):
+        target = device(x, y, z + (1, 3, 2)[i], c)
+        if from_units:
+            piece = units.at[here, beta]
+            return copy(piece, piece, szb.at[i], rb.at[here], target)
+        piece = other.at[x, beta]
+        return copy(piece, piece, szb.at[i], rob, target)
+
+    def x_alpha(i, from_units):
+        target = device(x + (1, 3, 2)[i], y, z, c)
+        if from_units:
+            piece = units.at[here, alpha]
+            return copy(piece, piece, sxa.at[i], ra.at[here], target)
+        piece = other.at[x, alpha]
+        return copy(piece, piece, sxa.at[i], roa.at[x], target)
+
+    def z_alpha(t, s):
+        piece = units.at[s, alpha]
+        return copy(piece, piece, sza.at[t], ra.at[s], device(x, y, z + sign, c))
+
+    def y_alpha_own(t, s):
+        piece = units.at[s, alpha]
+        return copy(piece, piece, sya.at[t], ra.at[s], device(x, y + 2, z, c))
+
+    def y_alpha_other(t, xs, step):
+        s = slot(xs, y)
+        sems = sya if step == 1 else sya2
+        return copy(other.at[xs, alpha], units.at[s, alpha], sems.at[t], ra.at[s], device(x, y + step, z, c))
+
+    def y_beta_own():
+        piece = units.at[here, beta]
+        return copy(piece, piece, syb.at[2], rb.at[here], device(x, y + 2, z, c))
+
+    def y_beta_other(i):
+        return copy(other.at[x, beta], units.at[here, beta], syb.at[i], rb.at[here], device(x, y + (1, 3)[i], z, c))
+
+    def x_beta(n, s, step):
+        piece = units.at[s, beta]
+        return copy(piece, piece, sxb.at[n], rb.at[s], device(x + step, y, z, c))
+
+    @pl.when(is_own)
+    def _():
+        for i in range(3):
+            z_beta(i, True).start()
+            x_alpha(i, True).start()
+
+    @pl.when(is_other)
+    def _():
+        for i in range(3):
+            z_beta(i, False).start()
+            x_alpha(i, False).start()
+
+    out[...] = jnp.zeros_like(out)
+    w_copy.wait()
+
+    def step(t, carry):
+        a_x, a_y = (x + turn(t % 4)) % 4, (y + turn(t // 4)) % 4
+        b_x, b_y = (x + turn(t // 4)) % 4, (y + turn(t % 4)) % 4
+        a_slot, b_slot = slot(a_x, a_y), slot(b_x, b_y)
+        first = t < 4
+
+        @pl.when(first & is_other)
+        def _():
+            @pl.when(t > 0)
+            def _():
+                copy(other.at[a_x, alpha], other.at[a_x, alpha], s0, roa.at[a_x], core).wait_recv()
+
+            y_alpha_other(t, a_x, 1).start()
+            y_alpha_other(t, a_x, 3).start()
+
+        @pl.when(t == 0)
+        def _():
+            @pl.when(jnp.logical_not(is_other))
+            def _():
+                copy(other.at[x, beta], other.at[x, beta], s0, rob, core).wait_recv()
+
+            y_beta_other(0).start()
+            y_beta_other(1).start()
+
+        @pl.when(jnp.logical_not(is_own & (t == 0)))
+        def _():
+            copy(units.at[b_slot, beta], units.at[b_slot, beta], s0, rb.at[b_slot], core).wait_recv()
+
+        @pl.when(t == 0)
+        def _():
+            y_beta_own().start()
+
+        @pl.when(first)
+        def _():
+            x_beta(2 * t, b_slot, 1).start()
+            x_beta(2 * t + 1, b_slot, 3).start()
+
+        @pl.when((t == 6) | (t == 7))
+        def _():
+            x_beta(t + 2, b_slot, 3).start()
+
+        @pl.when((t == 8) | (t == 9))
+        def _():
+            x_beta(t + 2, b_slot, 1).start()
+
+        @pl.when(jnp.logical_not(is_own & (t == 0)))
+        def _():
+            copy(units.at[a_slot, alpha], units.at[a_slot, alpha], s0, ra.at[a_slot], core).wait_recv()
+
+        @pl.when(pi != 3)
+        def _():
+            z_alpha(t, a_slot).start()
+
+        @pl.when(is_own & first)
+        def _():
+            y_alpha_own(t, a_slot).start()
+
+        out[b_y % 2, beta, :] += jnp.dot(
+            units[b_slot, beta, :], w[4 * (b_y // 2) + b_x], preferred_element_type=jnp.float32
+        )
+        out[a_y % 2, alpha, :] += jnp.dot(
+            units[a_slot, alpha, :], w[4 * (a_y // 2) + a_x], preferred_element_type=jnp.float32
+        )
+        return carry
+
+    lax.fori_loop(0, 16, step, 0)
+
+    @pl.when(partner_zeta == 0)
+    def _():
+        to_units.wait_send()
+
+    @pl.when(partner_zeta == 2)
+    def _():
+        to_other.wait_send()
+
+    for i in range(2):
+        y_beta_other(i).wait_send()
+    y_beta_own().wait_send()
+
+    @pl.when(is_own | is_other)
+    def _():
+        for i in range(3):
+            z_beta(i, True).wait_send()
+            x_alpha(i, True).wait_send()
+
+    def drain_first(t, carry):
+        @pl.when(is_own | is_other)
+        def _():
+            y_alpha_own(t, here).wait_send()
+
+        @pl.when(is_other)
+        def _():
+            y_alpha_other(t, x, 3).wait_send()
+
+        return carry
+
+    lax.fori_loop(0, 4, drain_first, 0)
+
+    def drain_x(t, carry):
+        x_beta(t, here, 1).wait_send()
+        return carry
+
+    lax.fori_loop(0, 12, drain_x, 0)
+
+    @pl.when(pi != 3)
+    def _():
+        def drain_z(t, carry):
+            z_alpha(t, here).wait_send()
+            return carry
+
+        lax.fori_loop(0, 16, drain_z, 0)
+
+
+def rotate(act_rows, in_basis):
+    dma = pltpu.SemaphoreType.DMA
+    return pl.pallas_call(
+        rotate_kernel,
+        out_shape=jax.ShapeDtypeStruct((2, UNIT, COLS), jnp.float32),
+        in_specs=[pl.BlockSpec(memory_space=pltpu.VMEM), pl.BlockSpec(memory_space=pl.ANY)],
+        out_specs=pl.BlockSpec(memory_space=pltpu.VMEM),
+        scratch_shapes=[
+            pltpu.VMEM((16, UNIT, COLS), jnp.bfloat16),
+            pltpu.VMEM((4, UNIT, COLS), jnp.bfloat16),
+            pltpu.VMEM((8, COLS, COLS), jnp.bfloat16),
+            dma,
+            dma,
+            dma,
+            dma,
+            dma((16,)),
+            dma((16,)),
+            dma,
+            dma((4,)),
+            dma((3,)),
+            dma((3,)),
+            dma((12,)),
+            dma((3,)),
+            dma((4,)),
+            dma((4,)),
+            dma((16,)),
+        ],
+        compiler_params=pltpu.CompilerParams(
+            collective_id=0, has_side_effects=True, vmem_limit_bytes=56 * 2**20
+        ),
+        cost_estimate=pl.CostEstimate(flops=2 * 1280 * 4736 * 592, bytes_accessed=20 * 2**20, transcendentals=0),
+        name="rotate",
+    )(act_rows, in_basis.reshape(8, COLS, COLS))
 
 
 def on_device(
@@ -30,20 +317,14 @@
     tok_rows = train_act.shape[0]
     act_rows = jnp.concatenate([train_act, query_act], axis=0)
     grad_rows = jnp.concatenate([train_out_grad, query_out_grad], axis=0)
-    full_act = lax.all_gather(act_rows, "basis", axis=1, tiled=True)
-    rotated = jnp.dot(
-        full_act,
-        lax.all_gather(in_basis, "dp", axis=0, tiled=True),
-        preferred_element_type=jnp.float32,
-    )
-    rot_act = rotated.astype(jnp.bfloat16)
+    partial = rotate(act_rows, in_basis)
+    rotated = lax.psum(partial, "dp").astype(jnp.bfloat16).reshape(4, ROWS, COLS)
     contract = (((0,), (1,)), ((), ()))
     grad_term = lax.dot_general(out_basis, grad_rows, contract, preferred_element_type=jnp.float32)
     rot_grad = lax.psum(grad_term, "basis").astype(jnp.bfloat16)
-    query_rot_act, query_rot_grad = (
-        lax.all_gather(rot_act[tok_rows:], "dp", axis=0, tiled=True),
-        lax.all_gather(rot_grad[:, tok_rows:], "dp", axis=1, tiled=True),
-    )
+    query_rot_act = rotated[:, tok_rows:].reshape(4 * QTOK_DP, COLS)
+    train_rot_act = lax.dynamic_index_in_dim(rotated, lax.axis_index("dp"), keepdims=False)[:tok_rows]
+    query_rot_grad = lax.all_gather(rot_grad[:, tok_rows:], "dp", axis=1, tiled=True)
     hot_table = (pair_ids[None, :] == jnp.arange(PAIRS, dtype=jnp.int32)[:, None]).astype(
         jnp.bfloat16
     )
@@ -51,7 +332,7 @@
     query_rot = jnp.einsum("pdq,qj->pdj", masked, query_rot_act, preferred_element_type=jnp.float32)
     precond = (query_rot / (eigvals.astype(jnp.float32) + DAMPING)).astype(jnp.bfloat16)
     projected = jnp.einsum(
-        "pdj,tj->pdt", precond, rot_act[:tok_rows], preferred_element_type=jnp.float32
+        "pdj,tj->pdt", precond, train_rot_act, preferred_element_type=jnp.float32
     )
     token_score = jnp.sum(
         projected * rot_grad[:, :tok_rows].astype(jnp.float32)[None, :, :], axis=1

time: 727 us -> 548 us (0.75)
  waiting for transfers between devices: 296 us -> 0.02 us
  Pallas kernels: 0 us -> 98.5 us
  blocking collectives: 320 us -> 386 us
  local copies, waits for them, and re-layouts: 53.3 us -> 21.4 us
  matrix products: 33.5 us -> 17.7 us
    all_gather x2 -> x0, waiting for transfers between devices: 289 us -> none  [the longest x1 156 us: on_device(): lax.all_gather(in_basis, 'dp', axis=0, tiled=True)]
    pallas_call x0 -> x1, Pallas kernels: none -> 98.5 us  [rotate(): pl.pallas_call(rotate_kernel, out_shape=jax.ShapeDtypeStruct((2, UNIT, CO...]
    psum x0 -> x1, blocking collectives: none -> 76.3 us  [on_device(): lax.psum(partial, 'dp').astype(jnp.bfloat16).reshape(4, ROWS, COLS)]
    all_gather x1 -> x0, local copies, waits for them, and re-layouts: 16.8 us -> none  [on_device(): full_act = lax.all_gather(act_rows, 'basis', axis=1, tiled=True)]
    unnamed x15 -> x11, local copies, waits for them, and re-layouts: 27.6 us -> 11.6 us
    dot_general x2 -> x1, matrix products: 29.7 us -> 13.8 us  [on_device(): jnp.einsum('pdj,tj->pdt', precond, train_rot_act, preferred_element_type=...]
  transfers between devices with their start and end apart: 3 -> 1, of which waited for: 3 -> 0; matrix products, arithmetic and copies ran while one was open for 8% -> 5% of each run, Pallas kernels for 0% -> 18%
where the time goes in v1:
time: 548 us; the launch traced here: 547 us
  blocking collectives  386 us (70%)
  Pallas kernels  98.5 us (18%)
  local copies, waits for them, and re-layouts  21.4 us (4%)
  matrix products  17.7 us (3%)
  between operations  13.5 us (2%)
  other arithmetic  10.4 us (2%)
    psum x1, blocking collectives, on_device(): rot_grad = lax.psum(grad_term, 'basis').astype(jnp.bfloat16)  217 us
    pallas_call x1, Pallas kernels, rotate(): pl.pallas_call(rotate_kernel, out_shape=jax.ShapeDtypeStruct((2, UNIT, CO...  98.5 us
    psum x1, blocking collectives, on_device(): return lax.psum(partial_scores, 'basis') * score_scale  92.6 us
    psum x1, blocking collectives, on_device(): lax.psum(partial, 'dp').astype(jnp.bfloat16).reshape(4, ROWS, COLS)  76.3 us
    dot_general x1, matrix products, on_device(): jnp.einsum('pdj,tj->pdt', precond, train_rot_act, preferred_element_type=...  13.8 us
    unnamed x11, local copies, waits for them, and re-layouts  11.6 us
  transfers between devices with their start and end apart: 1, of which 0 were waited for; matrix products, arithmetic and copies ran while one was open for 5% of the time, Pallas kernels for 18%

profile of v1, /device:TPU:0, one launch (start us, length us, event | category | flops | bytes accessed | tf_op | source)
XLA Modules:
  0.0 547.3 jit_solution(3175535968930834672)
XLA Ops:
  6.5 0.0 copy-start
  6.5 0.0 all-gather.2.cloned.1.call-start
  6.5 0.9 copy.16
  7.4 0.3 copy-done
  7.7 3.6 convolution_bitcast_fusion
  11.3 0.0 copy-start.3
  11.3 216.9 %all-reduce.2 = bf16[3584,320]{0,1:T(8,128)(2,1)S(1)} all-reduce(f32[3584,320]{0,1:T(8,128)} %convolution_bitcast_fusion), channel_id=1, replica_groups=mesh['dp'=4,'basis'=32] {'basis'}, use_global_device_ids=true, to_apply=%region_0.0 | all-reduce | flops 1146880 | bytes 6881280 | tf_op jit(solution)/shard_map/psum | solution.py:324
  228.3 0.8 slice.20
  229.1 0.0 all-gather.2.cloned.1.call-update
  229.1 0.0 copy-done.3
  229.1 0.2 reduce-window.7
  229.3 1.2 copy.18
  230.4 0.0 copy-start.1
  230.5 9.3 %copy.19 = bf16[4736,592]{1,0:T(8,128)(2,1)} copy(bf16[4736,592]{0,1:T(8,128)(2,1)} %param.13) | data formatting | bytes 11214848 | tf_op args[4]
  239.8 0.0 copy-done.1
  239.8 0.8 pad_maximum_fusion.act
  240.6 98.5 %rotate.1 = f32[2,640,592]{2,1,0:T(8,128)} custom-call(bf16[320,592]{1,0:T(8,128)(2,1)} %pad_maximum_fusion.act, bf16[8,592,592]{2,1,0:T(8,128)(2,1)} %bitcast.19), custom_call_target="tpu_custom_call" | custom-call | flops 7177502720 | bytes 20971520 | tf_op jit(solution)/shard_map/rotate/pallas_call | solution.py:273
  339.1 76.3 %all-reduce.3 = bf16[2,640,592]{2,1,0:T(8,128)(2,1)} all-reduce(f32[2,640,592]{2,1,0:T(8,128)} %rotate.1), channel_id=1, replica_groups=mesh['dp'=4,'basis'=32] {'dp'}, use_global_device_ids=true, to_apply=%region_1.0 | all-reduce | flops 757760 | bytes 4546560 | tf_op jit(solution)/shard_map/psum | solution.py:321
  415.4 0.0 copy-start.2
  415.4 2.2 slice_convert_fusion
  417.6 5.1 copy.20
  422.7 1.0 slice.21
  423.7 0.0 copy-done.2
  423.7 6.6 %convert_add_fusion = f32[3584,592]{0,1:T(8,128)} fusion(bf16[3584,592]{0,1:T(8,128)(2,1)} %param.15), kind=kLoop, calls=%fused_computation.4 | loop fusion | flops 4243456 | bytes 12730368 | tf_op jit(solution)/shard_map/add | solution.py:333
  430.3 0.0 all-gather.2.cloned.1.call-done
  430.3 2.9 copy.17
  433.2 13.8 %multiply_reduce_fusion = bf16[4,256]{1,0:T(4,128)(2,1)S(1)} fusion(f32[3584,592]{0,1:T(8,128)} %convert_add_fusion, bf16[256,592,1]{1,0,2:T(8,128)(2,1)S(1)} %bitcast.22, f32[3584,256]{1,0:T(8,128)} %copy.20, bf16[4,256]{1,0:T(4,128)(2,1)S(1)} %fusion.12, bf16[3584,256]{1,0:T(8,128)(2,1)S(1)} %copy.17, bf16[4,320,592]{2,1,0:T(8,128)(2,1)} %bitcast.21, ...), kind=kOutput, calls=%fused_computation.2 | convolution fusion | flops 8718580736 | bytes 14626820 | tf_op jit(solution)/shard_map/pdj,tj->pdt/dot_general | solution.py:334
  447.1 0.2 fusion.14
  447.3 92.6 %psum.23 = f32[4,4]{1,0:T(4,128)S(1)} all-reduce(f32[4,4]{1,0:T(4,128)S(1)} %fusion.14), channel_id=1, replica_groups=mesh['dp'=4,'basis'=32] {'basis'}, use_global_device_ids=true, to_apply=%region_4.5 | all-reduce | flops 16 | bytes 128 | tf_op jit(solution)/shard_map/psum | solution.py:349
  539.9 0.6 broadcast_multiply_fusion
  (2 shorter events, 0.0 us)
Async XLA Ops:
  6.5 1.2 copy-start
  6.5 423.8 %all-gather.2.cloned.1.call-start = ((), (), s32[]{:S(2)}) async-start(), calls=%async_computation | async-start | bytes 2293760 | tf_op jit(solution)/shard_map/all_gather | solution.py:327
  11.3 217.8 %copy-start.3 = (s32[1,4]{1,0:T(1,128)S(1)}, s32[1,4]{1,0:T(1,128)}, u32[]{:S(2)}) copy-start(s32[1,4]{1,0:T(1,128)} %param.17) | copy-start | bytes 52
  230.4 9.3 %copy-start.1 = (bf16[64,592]{1,0:T(8,128)(2,1)S(1)}, bf16[64,592]{1,0:T(8,128)(2,1)}, u32[]{:S(2)}) copy-start(bf16[64,592]{1,0:T(8,128)(2,1)} %param.11) | copy-start | bytes 227332
  415.4 8.4 %copy-start.2 = (s32[256]{0:T(256)S(1)}, s32[256]{0:T(256)}, u32[]{:S(2)}) copy-start(s32[256]{0:T(256)} %param.16) | copy-start | bytes 3076
Sparse Core Ops, SparseCore 0:
  229.2 23.7 all-gather.1

commit v2 on v0

v2 whole, which is shorter than its diff:
```python
import functools
import math

import jax
import jax.numpy as jnp
from jax import lax
from jax.experimental import pallas as pl
from jax.experimental.pallas import tpu as pltpu
from jax.sharding import PartitionSpec as P

D = 3584
FF = 18944
PAIRS = 4
SEQ_DP = 4
TOK_DP = 256
QTOK_DP = 64
ROWS = TOK_DP + QTOK_DP
COLS = FF // 32
DEPTH = FF // 4
FEAT = D // 32
QUART = D // 4
LANES = 2 * ROWS
TRAIN = 2 * TOK_DP
CHUNK = ROWS // 4

DAMPING = 0.5
SCALE = SEQ_DP / math.sqrt(D * FF * TOK_DP * QTOK_DP)
MESH = pl.DeviceIdType.MESH
F32, BF16 = jnp.float32, jnp.bfloat16

RB = 336
OTHER = (1, 3, 2)


def place():
    dp, b = lax.axis_index("dp"), lax.axis_index("basis")
    return b % 4, ((b // 4) % 2) * 2 + dp // 2, b // 8, dp % 2


def device(x, y, z, c):
    x, y, z = (x + 4) % 4, (y + 4) % 4, (z + 4) % 4
    return ((y % 2) * 2 + c, z * 8 + (y // 2) * 4 + x)


class Sems:
    def __init__(self):
        self.used = 0

    def take(self, n=1):
        self.used += n
        return self.used - n


N_SEMS = 200


def kernel(
    train_t, query, train_g_t, query_g, pid, lengths, w_hbm, eig_hbm, ob_hbm, out,
    units, other, w, acc, query_t, query_in, eig, recip,
    og_tok, og_feat, ob, g_sum, g_part, g_rz, g_yb, g_ry, g_full, g_train_t,
    sum_in, chip_out, chip_in, rot, precond, tok, tok_in, tok_y, tok_yin, red_x, red_z, red_y,
    sems,
):
    x, y, z, c = place()
    k = y % 2
    d = 2 * k + c
    zeta = (z - d + 4) % 4
    sign = 1 - 2 * c
    pi = (sign * zeta + 4) % 4
    is_own, is_other = zeta == 0, zeta == 2
    names = Sems()

    def sem(base, i=0):
        return sems.at[base + i]

    def slot(xs, ys):
        return ((xs + 4) % 4) * 4 + (ys + 4) % 4

    def unit(xs, ys, low, count, lanes=None):
        xs, ys = (xs + 4) % 4, (ys + 4) % 4
        rows = pl.ds(pl.multiple_of(COLS * (4 * (ys // 2) + xs) + low, 16), count)
        return units.at[ys % 2, rows] if lanes is None else units.at[ys % 2, rows, lanes]

    def beta(xs, ys):
        return unit(xs, ys, 0, RB)

    def alpha(xs, ys):
        return unit(xs, ys, RB, COLS - RB)

    def copy(src, dst, send, recv, target):
        return pltpu.make_async_remote_copy(
            src_ref=src, dst_ref=dst, send_sem=send, recv_sem=recv, device_id=target, device_id_type=MESH
        )

    partners = [device(x + o, y, z, c) for o in OTHER]
    partners += [device(x, y + o, z, c) for o in OTHER]
    partners += [device(x, y, z + o, c) for o in OTHER]
    core = device(x, y, z, 1 - c)
    partners += [core]
    mate = device(x, y + 1 - 2 * k, z, c)

    def landed(dst, recv):
        copy(dst, dst, sem(dummy), recv, core).wait_recv()

    sent = []

    def send(src, dst, s, r, target):
        cp = copy(src, dst, s, r, target)
        cp.start()
        sent.append(cp)

    dummy = names.take()
    s_w, s_eig, s_ob, s_own = names.take(), names.take(), names.take(), names.take()
    s_step, r_step = names.take(2), names.take(2)
    r_b, r_a, r_ob, r_oa = names.take(16), names.take(16), names.take(), names.take(4)
    s_zb, s_yb, s_xb = names.take(3), names.take(3), names.take(12)
    s_xa, s_ya, s_ya2, s_za = names.take(3), names.take(4), names.take(4), names.take(16)

    w_copy = pltpu.make_async_copy(w_hbm, w, sem(s_w))
    w_copy.start()
    quarter = pl.ds(pl.multiple_of(d * QUART, 128), QUART)
    ob_copy = pltpu.make_async_copy(ob_hbm.at[:, quarter], ob.at[x], sem(s_ob))
    ob_copy.start()
    eig_copy = pltpu.make_async_copy(eig_hbm.at[:, quarter], eig, sem(s_eig))
    eig_copy.start()

    barrier = pltpu.get_barrier_semaphore()
    for p in partners:
        pl.semaphore_signal(barrier, inc=1, device_id=p, device_id_type=MESH)
    pl.semaphore_wait(barrier, len(partners))

    turned = query[...].astype(F32).T.astype(BF16)
    nothing = jnp.zeros_like(turned)
    query_t[...] = jnp.concatenate(
        [jnp.where(c == 0, turned, nothing), jnp.where(c == 1, turned, nothing)], axis=1
    )
    og_tok[d, 0:TOK_DP, :] = train_g_t[...].astype(F32).T.astype(BF16)
    og_tok[d, TOK_DP:, :] = query_g[...]

    gs_c, gr_c = names.take(), names.take()
    send(og_tok.at[d], og_tok.at[d], sem(gs_c), sem(gr_c), core)

    mine = pl.ds(pl.multiple_of(c * TOK_DP, 128), TOK_DP)
    theirs = pl.ds(pl.multiple_of((1 - c) * TOK_DP, 128), TOK_DP)
    tail = pl.ds(TRAIN, LANES - TRAIN)
    partner_zeta = (zeta - sign + 4) % 4
    to_units = copy(train_t, unit(x, y, 0, COLS, mine), sem(s_step), sem(r_step), core)
    to_other = copy(train_t, other.at[x, :, mine], sem(s_step), sem(r_step), core)
    to_query = copy(query_t, query_in, sem(s_step, 1), sem(r_step, 1), core)

    @pl.when(partner_zeta == 0)
    def _():
        to_units.start()

    @pl.when(partner_zeta == 2)
    def _():
        to_other.start()

    @pl.when((partner_zeta == 0) | (partner_zeta == 2))
    def _():
        to_query.start()

    def z_beta(i, own):
        piece = beta(x, y) if own else other.at[x, pl.ds(0, RB)]
        return copy(piece, piece, sem(s_zb, i), sem(r_b, slot(x, y)) if own else sem(r_ob), device(x, y, z + OTHER[i], c))

    def x_alpha(i, own):
        piece = alpha(x, y) if own else other.at[x, pl.ds(RB, COLS - RB)]
        return copy(piece, piece, sem(s_xa, i), sem(r_a, slot(x, y)) if own else sem(r_oa, x), device(x + OTHER[i], y, z, c))

    def z_alpha(t, xs, ys):
        piece = alpha(xs, ys)
        return copy(piece, piece, sem(s_za, t), sem(r_a, slot(xs, ys)), device(x, y, z + sign, c))

    def y_alpha_own(i, xs):
        piece = alpha(xs, y)
        return copy(piece, piece, sem(s_ya, i), sem(r_a, slot(xs, y)), device(x, y + 2, z, c))

    def y_alpha_other(i, xs, step):
        src = other.at[xs, pl.ds(RB, COLS - RB)]
        return copy(src, alpha(xs, y), sem(s_ya if step == 1 else s_ya2, i), sem(r_a, slot(xs, y)), device(x, y + step, z, c))

    def y_beta_own():
        piece = beta(x, y)
        return copy(piece, piece, sem(s_yb, 2), sem(r_b, slot(x, y)), device(x, y + 2, z, c))

    def y_beta_other(i):
        src = other.at[x, pl.ds(0, RB)]
        return copy(src, beta(x, y), sem(s_yb, i), sem(r_b, slot(x, y)), device(x, y + OTHER[i], z, c))

    def x_beta(n, xs, ys, step):
        piece = beta(xs, ys)
        return copy(piece, piece, sem(s_xb, n), sem(r_b, slot(xs, ys)), device(x + step, y, z, c))

    def gather_step(dst_mine, dst_theirs, dst_tail):
        own = pltpu.make_async_copy(train_t, dst_mine, sem(s_own))
        own.start()
        own.wait()
        landed(query_in, sem(r_step, 1))
        dst_tail[...] = query_t[...] + query_in[...]
        landed(dst_theirs, sem(r_step))

    @pl.when(is_own)
    def _():
        gather_step(unit(x, y, 0, COLS, mine), unit(x, y, 0, COLS, theirs), unit(x, y, 0, COLS, tail))
        for i in range(3):
            z_beta(i, True).start()
            x_alpha(i, True).start()

    @pl.when(is_other)
    def _():
        gather_step(other.at[x, :, mine], other.at[x, :, theirs], other.at[x, :, tail])
        for i in range(3):
            z_beta(i, False).start()
            x_alpha(i, False).start()
        y_alpha_other(0, x, 1).start()
        y_alpha_other(0, x, 3).start()

    @pl.when(is_own)
    def _():
        y_alpha_own(0, x).start()

    gs_y, gr_y = names.take(2), names.take(2)
    landed(og_tok.at[2 * k + 1 - c], sem(gr_c))
    send(og_tok.at[2 * k], og_tok.at[2 * k], sem(gs_y), sem(gr_y), mate)
    send(og_tok.at[2 * k + 1], og_tok.at[2 * k + 1], sem(gs_y, 1), sem(gr_y, 1), mate)
    ob_copy.wait()
    gs_ob, gr_ob = names.take(3), names.take(4)
    for i, o in enumerate(OTHER):
        send(ob.at[x], ob.at[x], sem(gs_ob, i), sem(gr_ob, x), device(x + o, y, z, c))

    ALPHA = [(0, 0), (1, 0), (3, 0), (2, 0), (0, 2), (0, 1), (0, 3), (1, 2), (3, 2), (2, 2)]
    ALPHA += [(1, 1), (1, 3), (3, 1), (3, 3), (2, 1), (2, 3)]
    BETA = (0, 2, 1, 3)

    def on_x(o):
        return (x + o) % 4

    def on_y(o):
        return (y + o) % 4

    def alphas(first, last):
        for t in range(first, last):
            dx, dy = ALPHA[t]
            xs, ys = on_x(dx), on_y(dy)
            if (dx, dy) == (0, 0):

                @pl.when(jnp.logical_not(is_own))
                def _():
                    landed(alpha(xs, ys), sem(r_a, slot(xs, ys)))
            else:
                landed(alpha(xs, ys), sem(r_a, slot(xs, ys)))

            @pl.when(pi != 3)
            def _():
                z_alpha(t, xs, ys).start()

    def own_beta(i):
        ys = on_y(BETA[i])
        if i == 0:

            @pl.when(jnp.logical_not(is_own))
            def _():
                landed(beta(x, ys), sem(r_b, slot(x, ys)))
        else:
            landed(beta(x, ys), sem(r_b, slot(x, ys)))
        x_beta(2 * i, x, ys, 1).start()
        x_beta(2 * i + 1, x, ys, 3).start()

    def side_beta(i):
        ys = on_y(BETA[i])
        order = ((3, 1), (1, 3))[i % 2]
        for n, dx in enumerate(order):
            landed(beta(on_x(dx), ys), sem(r_b, slot(on_x(dx), ys)))
            if n == 0:
                x_beta(8 + i, on_x(dx), ys, 4 - dx).start()

    def far_beta(i):
        ys = on_y(BETA[i])
        landed(beta(on_x(2), ys), sem(r_b, slot(on_x(2), ys)))

    own_beta(0)
    y_beta_own().start()

    @pl.when(jnp.logical_not(is_other))
    def _():
        landed(other.at[x, pl.ds(0, RB)], sem(r_ob))

    y_beta_other(0).start()
    y_beta_other(1).start()
    alphas(0, 2)

    landed(og_tok.at[2 * (1 - k)], sem(gr_y))
    landed(og_tok.at[2 * (1 - k) + 1], sem(gr_y, 1))
    gs_f, gr_f = names.take(3), names.take(4)
    for i, o in enumerate(OTHER):
        q = (x + o) % 4
        send(og_tok.at[q], og_feat.at[x], sem(gs_f, i), sem(gr_f, x), device(x + o, y, z, c))
    og_feat[x] = og_tok[x]

    own_beta(1)
    alphas(2, 4)

    @pl.when(is_own)
    def _():
        for i, dx in enumerate(OTHER):
            y_alpha_own(i + 1, on_x(dx)).start()

    @pl.when(is_other)
    def _():
        for i, dx in enumerate(OTHER):
            landed(other.at[on_x(dx), pl.ds(RB, COLS - RB)], sem(r_oa, on_x(dx)))
            y_alpha_other(i + 1, on_x(dx), 1).start()
            y_alpha_other(i + 1, on_x(dx), 3).start()

    side_beta(0)
    for o in OTHER:
        xs = (x + o) % 4
        landed(og_feat.at[xs], sem(gr_f, xs))
        landed(ob.at[xs], sem(gr_ob, xs))

    def feature_block(i, carry):
        g_sum[...] += jnp.dot(og_feat[i], ob[i], preferred_element_type=F32)
        return carry

    g_sum[...] = jnp.zeros_like(g_sum)
    lax.fori_loop(0, 4, feature_block, 0)
    g_part[...] = g_sum[...].astype(BF16)

    def chunk(zz):
        return pl.ds(pl.multiple_of(((zz + 4) % 4) * CHUNK, 16), CHUNK)

    gs_z, gr_z = names.take(3), names.take(4)
    for i, o in enumerate(OTHER):
        send(g_part.at[chunk(z + o)], g_rz.at[z], sem(gs_z, i), sem(gr_z, z), device(x, y, z + o, c))

    eig_copy.wait()
    recip[...] = 1.0 / (eig[...].astype(F32) + DAMPING)

    own_beta(2)
    own_beta(3)
    alphas(4, 5)
    side_beta(1)
    alphas(5, 6)
    total = g_sum[chunk(z), :]
    for o in OTHER:
        zz = (z + o) % 4
        landed(g_rz.at[zz], sem(gr_z, zz))
        total = total + g_rz[zz].astype(F32)
    g_sum[chunk(z), :] = total
    g_yb[...] = total.astype(BF16)
    gs_h, gr_h = names.take(), names.take()
    send(g_yb, g_ry, sem(gs_h), sem(gr_h), device(x, y + 2, z, c))

    alphas(6, 8)
    landed(g_ry, sem(gr_h))
    g_full[x, chunk(z), :] = (g_sum[chunk(z), :] + g_ry[...].astype(F32)).astype(BF16)
    gs_g, gr_g = names.take(3), names.take(4)
    for i, o in enumerate(OTHER):
        piece = g_full.at[x, chunk(z)]
        send(piece, piece, sem(gs_g, i), sem(gr_g, z), device(x, y, z + o, c))

    side_beta(2)
    alphas(8, 9)
    for o in OTHER:
        zz = (z + o) % 4
        landed(g_full.at[x, chunk(zz)], sem(gr_g, zz))
    gs_x, gr_x = names.take(4), names.take(4)
    half_a, half_b = pl.ds(0, ROWS // 2), pl.ds(ROWS // 2, ROWS // 2)
    right, left = device(x + 1, y, z, c), device(x + 3, y, z, c)
    send(g_full.at[x], g_full.at[x], sem(gs_x), sem(gr_x), right)
    send(g_full.at[x], g_full.at[x], sem(gs_x, 1), sem(gr_x, 1), left)

    alphas(9, 10)
    far_beta(0)
    far_beta(1)
    x_prev, x_next, x_far = (x + 3) % 4, (x + 1) % 4, (x + 2) % 4
    w_copy.wait()

    def product(yl):
        acc[yl] = jnp.dot(w[:, 4608:], units[yl, 4608:, :], preferred_element_type=F32)

        def body(i, carry):
            rows = pl.ds(pl.multiple_of(i * 768, 128), 768)
            acc[yl] += jnp.dot(w[:, rows], units[yl, rows, :], preferred_element_type=F32)
            return carry

        lax.fori_loop(0, 6, body, 0)

    s_c1, r_c1, s_m, r_m, s_c2, r_c2 = (names.take() for _ in range(6))

    early, late = k, 1 - k
    sums_early = c == early

    def to_core(yl):
        return copy(acc.at[yl], sum_in, sem(s_c1), sem(r_c1), core)

    def to_mate():
        return copy(chip_out, chip_in, sem(s_m), sem(r_m), mate)

    def back_to_core(yl):
        return copy(rot.at[yl], rot.at[yl], sem(s_c2), sem(r_c2), core)

    def chip_sum(yl):
        landed(sum_in, sem(r_c1))
        acc[yl] += sum_in[...]
        chip_out[...] = acc[yl].astype(BF16)
        to_mate().start()

    def finish(yl):
        landed(chip_in, sem(r_m))
        rot[yl] = (acc[yl] + chip_in[...].astype(F32)).astype(BF16)
        back_to_core(yl).start()

    product(early)

    @pl.when(jnp.logical_not(sums_early))
    def _():
        to_core(early).start()

    alphas(10, 12)
    side_beta(3)
    landed(g_full.at[x_prev], sem(gr_x))
    send(g_full.at[x_prev, half_a], g_full.at[x_prev, half_a], sem(gs_x, 2), sem(gr_x, 2), right)
    landed(g_full.at[x_next], sem(gr_x, 1))
    send(g_full.at[x_next, half_b], g_full.at[x_next, half_b], sem(gs_x, 3), sem(gr_x, 3), left)

    @pl.when(sums_early)
    def _():
        chip_sum(early)

    alphas(12, 16)
    far_beta(2)
    far_beta(3)
    product(late)

    @pl.when(sums_early)
    def _():
        to_core(late).start()

    landed(g_full.at[x_far, half_a], sem(gr_x, 2))
    landed(g_full.at[x_far, half_b], sem(gr_x, 3))

    def transpose(q, carry):
        g_train_t[q] = g_full[q, 0:TOK_DP, :].astype(F32).T.astype(BF16)
        return carry

    lax.fori_loop(0, 4, transpose, 0)

    @pl.when(jnp.logical_not(sums_early))
    def _():
        chip_sum(late)
        finish(late)

    @pl.when(sums_early)
    def _():
        finish(early)
        landed(rot.at[late], sem(r_c2))

    @pl.when(jnp.logical_not(sums_early))
    def _():
        landed(rot.at[early], sem(r_c2))

    query_rot = jnp.concatenate([rot[0, :, TRAIN:], rot[1, :, TRAIN:]], axis=1).astype(F32)
    query_grad = jnp.concatenate([g_full[q, TOK_DP:, :] for q in range(4)], axis=0)
    for p in range(PAIRS):
        masked = jnp.where(pid[...] == p, query_rot, 0.0).astype(BF16)
        precond[p] = (jnp.dot(masked, query_grad, preferred_element_type=F32) * recip[...]).astype(BF16)

    def token_scores(q, carry):
        lanes = pl.ds(pl.multiple_of((q % 2) * TOK_DP, 128), TOK_DP)
        train = rot[q // 2, :, lanes].astype(F32)
        rows = []
        for p in range(PAIRS):
            projected = jnp.dot(precond[p], g_train_t[q], preferred_element_type=F32)
            rows.append(jnp.sum(projected * train, axis=0, keepdims=True))
        rows.append(jnp.zeros((8 - PAIRS, TOK_DP), F32))
        tok[q % 2, q // 2] = jnp.concatenate(rows, axis=0)
        return carry

    lax.fori_loop(0, 4, token_scores, 0)

    ts_c, tr_c, ts_y, tr_y = (names.take() for _ in range(4))
    send(tok.at[1 - c], tok_in, sem(ts_c), sem(tr_c), core)
    landed(tok_in, sem(tr_c))
    tok_y[...] = tok[c] + tok_in[...]
    send(tok_y.at[1 - k], tok_yin, sem(ts_y), sem(tr_y), mate)
    landed(tok_yin, sem(tr_y))
    scores = tok_y[k] + tok_yin[...]

    lane = lax.broadcasted_iota(jnp.int32, (8, TOK_DP), 1)
    column = lax.broadcasted_iota(jnp.int32, (8, 128), 1)
    result = jnp.zeros((8, 128), F32)
    start = jnp.int32(0)
    for n in range(SEQ_DP):
        end = start + lengths[0, n]
        part = jnp.sum(jnp.where((lane >= start) & (lane < end), scores, 0.0), axis=1, keepdims=True)
        result = jnp.where(column == n, part, result)
        start = end

    for buf, at, target in (
        (red_x, x, lambda o: device(x + o, y, z, c)),
        (red_z, z, lambda o: device(x, y, z + o, c)),
    ):
        s_red, r_red = names.take(3), names.take(4)
        buf[at] = result
        for i, o in enumerate(OTHER):
            send(buf.at[at], buf.at[at], sem(s_red, i), sem(r_red, at), target(o))
        for o in OTHER:
            landed(buf.at[(at + o) % 4], sem(r_red, (at + o) % 4))
        result = (buf[0] + buf[1]) + (buf[2] + buf[3])
    s_red, r_red = names.take(), names.take()
    red_y[y // 2] = result
    send(red_y.at[y // 2], red_y.at[y // 2], sem(s_red), sem(r_red), device(x, y + 2, z, c))
    landed(red_y.at[1 - y // 2], sem(r_red))
    out[...] = (red_y[0] + red_y[1]) * SCALE

    for cp in sent:
        cp.wait_send()

    @pl.when(partner_zeta == 0)
    def _():
        to_units.wait_send()

    @pl.when(partner_zeta == 2)
    def _():
        to_other.wait_send()

    @pl.when((partner_zeta == 0) | (partner_zeta == 2))
    def _():
        to_query.wait_send()

    for i in range(2):
        y_beta_other(i).wait_send()
    y_beta_own().wait_send()

    @pl.when(is_own | is_other)
    def _():
        for i in range(3):
            z_beta(i, True).wait_send()
            x_alpha(i, True).wait_send()
        for i in range(4):
            y_alpha_own(i, x).wait_send()

    @pl.when(is_other)
    def _():
        for i in range(4):
            y_alpha_other(i, x, 3).wait_send()

    def drain_x(n, carry):
        x_beta(n, x, y, 1).wait_send()
        return carry

    lax.fori_loop(0, 12, drain_x, 0)

    @pl.when(pi != 3)
    def _():
        def drain_z(t, carry):
            z_alpha(t, x, y).wait_send()
            return carry

        lax.fori_loop(0, 16, drain_z, 0)

    to_core(0).wait_send()
    to_mate().wait_send()
    back_to_core(0).wait_send()

    assert names.used <= N_SEMS


def fused(train_t, query, train_g_t, query_g, pid, lengths, in_basis_t, eig_t, out_basis):
    vmem, hbm = pl.BlockSpec(memory_space=pltpu.VMEM), pl.BlockSpec(memory_space=pl.ANY)
    smem = pl.BlockSpec(memory_space=pltpu.SMEM)

    def v(shape, dtype=BF16):
        return pltpu.VMEM(shape, dtype)

    return pl.pallas_call(
        kernel,
        out_shape=jax.ShapeDtypeStruct((8, 128), F32),
        in_specs=[vmem, vmem, vmem, vmem, vmem, smem, hbm, hbm, hbm],
        out_specs=vmem,
        scratch_shapes=[
            v((2, DEPTH, LANES)),
            v((4, COLS, LANES)),
            v((COLS, DEPTH)),
            v((2, COLS, LANES), F32),
            v((COLS, LANES - TRAIN)),
            v((COLS, LANES - TRAIN)),
            v((COLS, QUART)),
            v((COLS, QUART), F32),
            v((4, ROWS, FEAT)),
            v((4, ROWS, FEAT)),
            v((4, FEAT, QUART)),
            v((ROWS, QUART), F32),
            v((ROWS, QUART)),
            v((4, CHUNK, QUART)),
            v((CHUNK, QUART)),
            v((CHUNK, QUART)),
            v((4, ROWS, QUART)),
            v((4, QUART, TOK_DP)),
            v((COLS, LANES), F32),
            v((COLS, LANES)),
            v((COLS, LANES)),
            v((2, COLS, LANES)),
            v((PAIRS, COLS, QUART)),
            v((2, 2, 8, TOK_DP), F32),
            v((2, 8, TOK_DP), F32),
            v((2, 8, TOK_DP), F32),
            v((8, TOK_DP), F32),
            v((4, 8, 128), F32),
            v((4, 8, 128), F32),
            v((2, 8, 128), F32),
            pltpu.SemaphoreType.DMA((N_SEMS,)),
        ],
        compiler_params=pltpu.CompilerParams(
            collective_id=0, has_side_effects=True, vmem_limit_bytes=60 * 2**20
        ),
        cost_estimate=pl.CostEstimate(
            flops=2 * 1280 * 4736 * 592 + 8 * 896 * 592 * 1280, bytes_accessed=20 * 2**20, transcendentals=0
        ),
        name="influence",
    )(train_t, query, train_g_t, query_g, pid, lengths, in_basis_t, eig_t, out_basis)


def on_device(
    train_act,
    train_out_grad,
    query_act,
    query_out_grad,
    in_basis,
    out_basis,
    eigvals,
    pair_ids,
    seq_lengths,
):
    scores = fused(
        train_act.T,
        query_act,
        train_out_grad.T,
        query_out_grad,
        pair_ids[None, :],
        seq_lengths,
        in_basis.T,
        eigvals.T,
        out_basis,
    )
    return scores[:PAIRS, :SEQ_DP]


def solution(mesh):
    in_specs = (
        P("dp", "basis"),
        P("dp", "basis"),
        P("dp", "basis"),
        P("dp", "basis"),
        P("dp", "basis"),
        P("basis", None),
        P(None, "basis"),
        P(),
        P("dp", None),
    )
    out_specs = P(None, "dp")
    return jax.shard_map(
        on_device, mesh=mesh, in_specs=in_specs, out_specs=out_specs, check_vma=False
    )
```

time: 727 us -> 184 us (0.25)
  blocking collectives: 320 us -> 0 us
  waiting for transfers between devices: 296 us -> 0 us
  Pallas kernels: 0 us -> 182 us
  local copies, waits for them, and re-layouts: 53.3 us -> 1.26 us
  matrix products: 33.5 us -> 0 us
  between operations: 13.2 us -> 0.01 us
  other arithmetic: 10.5 us -> 0 us
    psum x2 -> x0, blocking collectives: 313 us -> none  [the longest x1 217 us: on_device(): rot_grad = lax.psum(grad_term, 'basis').astype(jnp.bfloat16)]
    all_gather x3 -> x0, waiting for transfers between devices: 295 us -> none  [the longest x1 156 us: on_device(): lax.all_gather(in_basis, 'dp', axis=0, tiled=True)]
    pallas_call x0 -> x1, Pallas kernels: none -> 182 us  [fused(): pl.pallas_call(kernel, out_shape=jax.ShapeDtypeStruct((8, 128), F32), in_...]
    dot_general x4 -> x0, matrix products: 33.5 us -> none  [the longest x1 15.8 us: on_device(): jnp.dot(full_act, lax.all_gather(in_basis, 'dp', axis=0, tiled=True), pre...]
    unnamed x15 -> x0, local copies, waits for them, and re-layouts: 27.6 us -> none
    all_gather x2 -> x0, local copies, waits for them, and re-layouts: 19.7 us -> none  [the longest x1 16.8 us: on_device(): full_act = lax.all_gather(act_rows, 'basis', axis=1, tiled=True)]
  transfers between devices with their start and end apart: 3 -> 0, of which waited for: 3 -> 0; matrix products, arithmetic and copies ran while one was open for 8% -> 0% of each run, Pallas kernels for 0% -> 0%
where the time goes in v2:
time: 184 us; the launch traced here: 183 us
  Pallas kernels  182 us (99%)
    pallas_call x1, Pallas kernels, fused(): pl.pallas_call(kernel, out_shape=jax.ShapeDtypeStruct((8, 128), F32), in_...  182 us

profile of v2, /device:TPU:0, one launch (start us, length us, event | category | flops | bytes accessed | tf_op | source)
XLA Modules:
  0.0 183.1 jit_solution(12452143283002243874)
XLA Ops:
  0.0 181.8 %influence.1 = f32[8,128]{1,0:T(8,128)} custom-call(bf16[592,256]{1,0:T(8,128)(2,1)} %bitcast.7, bf16[64,592]{1,0:T(8,128)(2,1)} %query.1, bf16[112,256]{1,0:T(8,128)(2,1)} %bitcast.8, bf16[64,112]{1,0:T(8,128)(2,1)} %query_g.1, s32[1,256]{1,0:T(1,128)} %bitcast.9, s32[1,4]{1,0:T(1,128)} %lengths.1, bf16[592,4736]{1,0:T(8,128)(2,1)} %bitcast.5, ...), custom_call_target="tpu_custom_call" | custom-call | flops 12609126400 | bytes 20971520 | tf_op jit(solution)/shard_map/influence/pallas_call | solution.py:578
  181.9 1.3 slice.3

commit v3 on v2

--- a/solution.py
+++ b/solution.py
@@ -28,8 +28,12 @@
 MESH = pl.DeviceIdType.MESH
 F32, BF16 = jnp.float32, jnp.bfloat16
 
-RB = 336
+RB = 368
+PARTS = 2
+RA = (COLS - RB) // PARTS
 OTHER = (1, 3, 2)
+CHUNKS = ((TRAIN, LANES - TRAIN), (0, TOK_DP), (TOK_DP, TOK_DP))
+COPIES = ((0,), (1, 2), (3, 4))
 
 
 def place():
@@ -51,14 +55,14 @@
         return self.used - n
 
 
-N_SEMS = 200
+N_SEMS = 256
 
 
 def kernel(
     train_t, query, train_g_t, query_g, pid, lengths, w_hbm, eig_hbm, ob_hbm, out,
     units, other, w, acc, query_t, query_in, eig, recip,
     og_tok, og_feat, ob, g_sum, g_part, g_rz, g_yb, g_ry, g_full, g_train_t,
-    sum_in, chip_out, chip_in, rot, precond, tok, tok_in, tok_y, tok_yin, red_x, red_z, red_y,
+    sum_in, chip_out, chip_in, rot, precond, tok, tok_in, red_x, red_z,
     sems,
 ):
     x, y, z, c = place()
@@ -84,8 +88,11 @@
     def beta(xs, ys):
         return unit(xs, ys, 0, RB)
 
-    def alpha(xs, ys):
-        return unit(xs, ys, RB, COLS - RB)
+    def alpha(xs, ys, h):
+        return unit(xs, ys, RB + h * RA, RA)
+
+    def other_alpha(xs, h):
+        return other.at[xs, pl.ds(RB + h * RA, RA)]
 
     def copy(src, dst, send, recv, target):
         return pltpu.make_async_remote_copy(
@@ -96,7 +103,7 @@
     partners += [device(x, y + o, z, c) for o in OTHER]
     partners += [device(x, y, z + o, c) for o in OTHER]
     core = device(x, y, z, 1 - c)
-    partners += [core]
+    partners += [core] + [device(x, y + o, z, 1 - c) for o in OTHER]
     mate = device(x, y + 1 - 2 * k, z, c)
 
     def landed(dst, recv):
@@ -112,9 +119,9 @@
     dummy = names.take()
     s_w, s_eig, s_ob, s_own = names.take(), names.take(), names.take(), names.take()
     s_step, r_step = names.take(2), names.take(2)
-    r_b, r_a, r_ob, r_oa = names.take(16), names.take(16), names.take(), names.take(4)
+    r_b, r_a, r_ob, r_oa = names.take(16), names.take(16 * PARTS), names.take(), names.take(4 * PARTS)
     s_zb, s_yb, s_xb = names.take(3), names.take(3), names.take(12)
-    s_xa, s_ya, s_ya2, s_za = names.take(3), names.take(4), names.take(4), names.take(16)
+    s_xa, s_ya, s_ya2, s_za = (names.take(n * PARTS) for n in (3, 4, 4, 16))
 
     w_copy = pltpu.make_async_copy(w_hbm, w, sem(s_w))
     w_copy.start()
@@ -164,21 +171,25 @@
         piece = beta(x, y) if own else other.at[x, pl.ds(0, RB)]
         return copy(piece, piece, sem(s_zb, i), sem(r_b, slot(x, y)) if own else sem(r_ob), device(x, y, z + OTHER[i], c))
 
-    def x_alpha(i, own):
-        piece = alpha(x, y) if own else other.at[x, pl.ds(RB, COLS - RB)]
-        return copy(piece, piece, sem(s_xa, i), sem(r_a, slot(x, y)) if own else sem(r_oa, x), device(x + OTHER[i], y, z, c))
-
-    def z_alpha(t, xs, ys):
-        piece = alpha(xs, ys)
-        return copy(piece, piece, sem(s_za, t), sem(r_a, slot(xs, ys)), device(x, y, z + sign, c))
-
-    def y_alpha_own(i, xs):
-        piece = alpha(xs, y)
-        return copy(piece, piece, sem(s_ya, i), sem(r_a, slot(xs, y)), device(x, y + 2, z, c))
-
-    def y_alpha_other(i, xs, step):
-        src = other.at[xs, pl.ds(RB, COLS - RB)]
-        return copy(src, alpha(xs, y), sem(s_ya if step == 1 else s_ya2, i), sem(r_a, slot(xs, y)), device(x, y + step, z, c))
+    def got_alpha(xs, ys, h):
+        return sem(r_a, PARTS * slot(xs, ys) + h)
+
+    def x_alpha(i, own, h):
+        piece = alpha(x, y, h) if own else other_alpha(x, h)
+        got = got_alpha(x, y, h) if own else sem(r_oa, PARTS * x + h)
+        return copy(piece, piece, sem(s_xa, PARTS * i + h), got, device(x + OTHER[i], y, z, c))
+
+    def z_alpha(t, xs, ys, h):
+        piece = alpha(xs, ys, h)
+        return copy(piece, piece, sem(s_za, PARTS * t + h), got_alpha(xs, ys, h), device(x, y, z + sign, c))
+
+    def y_alpha_own(i, xs, h):
+        piece = alpha(xs, y, h)
+        return copy(piece, piece, sem(s_ya, PARTS * i + h), got_alpha(xs, y, h), device(x, y + 2, z, c))
+
+    def y_alpha_other(i, xs, step, h):
+        sent_by = sem(s_ya if step == 1 else s_ya2, PARTS * i + h)
+        return copy(other_alpha(xs, h), alpha(xs, y, h), sent_by, got_alpha(xs, y, h), device(x, y + step, z, c))
 
     def y_beta_own():
         piece = beta(x, y)
@@ -205,20 +216,24 @@
         gather_step(unit(x, y, 0, COLS, mine), unit(x, y, 0, COLS, theirs), unit(x, y, 0, COLS, tail))
         for i in range(3):
             z_beta(i, True).start()
-            x_alpha(i, True).start()
+            for h in range(PARTS):
+                x_alpha(i, True, h).start()
 
     @pl.when(is_other)
     def _():
         gather_step(other.at[x, :, mine], other.at[x, :, theirs], other.at[x, :, tail])
         for i in range(3):
             z_beta(i, False).start()
-            x_alpha(i, False).start()
-        y_alpha_other(0, x, 1).start()
-        y_alpha_other(0, x, 3).start()
+            for h in range(PARTS):
+                x_alpha(i, False, h).start()
+        for h in range(PARTS):
+            y_alpha_other(0, x, 1, h).start()
+            y_alpha_other(0, x, 3, h).start()
 
     @pl.when(is_own)
     def _():
-        y_alpha_own(0, x).start()
+        for h in range(PARTS):
+            y_alpha_own(0, x, h).start()
 
     gs_y, gr_y = names.take(2), names.take(2)
     landed(og_tok.at[2 * k + 1 - c], sem(gr_c))
@@ -243,17 +258,18 @@
         for t in range(first, last):
             dx, dy = ALPHA[t]
             xs, ys = on_x(dx), on_y(dy)
-            if (dx, dy) == (0, 0):
-
-                @pl.when(jnp.logical_not(is_own))
+            for h in range(PARTS):
+                if (dx, dy) == (0, 0):
+
+                    @pl.when(jnp.logical_not(is_own))
+                    def _():
+                        landed(alpha(xs, ys, h), got_alpha(xs, ys, h))
+                else:
+                    landed(alpha(xs, ys, h), got_alpha(xs, ys, h))
+
+                @pl.when(pi != 3)
                 def _():
-                    landed(alpha(xs, ys), sem(r_a, slot(xs, ys)))
-            else:
-                landed(alpha(xs, ys), sem(r_a, slot(xs, ys)))
-
-            @pl.when(pi != 3)
-            def _():
-                z_alpha(t, xs, ys).start()
+                    z_alpha(t, xs, ys, h).start()
 
     def own_beta(i):
         ys = on_y(BETA[i])
@@ -301,18 +317,6 @@
     own_beta(1)
     alphas(2, 4)
 
-    @pl.when(is_own)
-    def _():
-        for i, dx in enumerate(OTHER):
-            y_alpha_own(i + 1, on_x(dx)).start()
-
-    @pl.when(is_other)
-    def _():
-        for i, dx in enumerate(OTHER):
-            landed(other.at[on_x(dx), pl.ds(RB, COLS - RB)], sem(r_oa, on_x(dx)))
-            y_alpha_other(i + 1, on_x(dx), 1).start()
-            y_alpha_other(i + 1, on_x(dx), 3).start()
-
     side_beta(0)
     for o in OTHER:
         xs = (x + o) % 4
@@ -339,6 +343,21 @@
 
     own_beta(2)
     own_beta(3)
+
+    @pl.when(is_own)
+    def _():
+        for i, dx in enumerate(OTHER):
+            for h in range(PARTS):
+                y_alpha_own(i + 1, on_x(dx), h).start()
+
+    @pl.when(is_other)
+    def _():
+        for i, dx in enumerate(OTHER):
+            for h in range(PARTS):
+                landed(other_alpha(on_x(dx), h), sem(r_oa, PARTS * on_x(dx) + h))
+                y_alpha_other(i + 1, on_x(dx), 1, h).start()
+                y_alpha_other(i + 1, on_x(dx), 3, h).start()
+
     alphas(4, 5)
     side_beta(1)
     alphas(5, 6)
@@ -365,81 +384,112 @@
     for o in OTHER:
         zz = (z + o) % 4
         landed(g_full.at[x, chunk(zz)], sem(gr_g, zz))
-    gs_x, gr_x = names.take(4), names.take(4)
-    half_a, half_b = pl.ds(0, ROWS // 2), pl.ds(ROWS // 2, ROWS // 2)
-    right, left = device(x + 1, y, z, c), device(x + 3, y, z, c)
-    send(g_full.at[x], g_full.at[x], sem(gs_x), sem(gr_x), right)
-    send(g_full.at[x], g_full.at[x], sem(gs_x, 1), sem(gr_x, 1), left)
+    gs_x, gr_x, gs_v, gr_v = names.take(3), names.take(4), names.take(3), names.take(4)
+
+    def rows_of(yh):
+        return pl.ds(pl.multiple_of(yh * (ROWS // 2), 16), ROWS // 2)
+
+    low, high = rows_of(y // 2), rows_of(1 - y // 2)
+    for i, o in enumerate(OTHER):
+        send(g_full.at[x, low], g_full.at[x, low], sem(gs_x, i), sem(gr_x, x), device(x + o, y, z, c))
 
     alphas(9, 10)
     far_beta(0)
     far_beta(1)
-    x_prev, x_next, x_far = (x + 3) % 4, (x + 1) % 4, (x + 2) % 4
     w_copy.wait()
 
-    def product(yl):
-        acc[yl] = jnp.dot(w[:, 4608:], units[yl, 4608:, :], preferred_element_type=F32)
+    def lanes(n):
+        return pl.ds(*CHUNKS[n])
+
+    def product(yl, n):
+        ln = lanes(n)
+        acc[yl, :, ln] = jnp.dot(w[:, 4608:], units[yl, 4608:, ln], preferred_element_type=F32)
 
         def body(i, carry):
             rows = pl.ds(pl.multiple_of(i * 768, 128), 768)
-            acc[yl] += jnp.dot(w[:, rows], units[yl, rows, :], preferred_element_type=F32)
+            acc[yl, :, ln] += jnp.dot(w[:, rows], units[yl, rows, ln], preferred_element_type=F32)
             return carry
 
         lax.fori_loop(0, 6, body, 0)
 
-    s_c1, r_c1, s_m, r_m, s_c2, r_c2 = (names.take() for _ in range(6))
-
+    s_c1, r_c1, s_m, r_m, s_c2, r_c2 = (names.take(n) for n in (3, 3, 5, 5, 3, 3))
     early, late = k, 1 - k
     sums_early = c == early
-
-    def to_core(yl):
-        return copy(acc.at[yl], sum_in, sem(s_c1), sem(r_c1), core)
-
-    def to_mate():
-        return copy(chip_out, chip_in, sem(s_m), sem(r_m), mate)
-
-    def back_to_core(yl):
-        return copy(rot.at[yl], rot.at[yl], sem(s_c2), sem(r_c2), core)
-
-    def chip_sum(yl):
-        landed(sum_in, sem(r_c1))
-        acc[yl] += sum_in[...]
-        chip_out[...] = acc[yl].astype(BF16)
-        to_mate().start()
-
-    def finish(yl):
-        landed(chip_in, sem(r_m))
-        rot[yl] = (acc[yl] + chip_in[...].astype(F32)).astype(BF16)
-        back_to_core(yl).start()
-
-    product(early)
-
-    @pl.when(jnp.logical_not(sums_early))
-    def _():
-        to_core(early).start()
+    sums_late = jnp.logical_not(sums_early)
+
+    def along_y(m):
+        return pl.ds(((m + 4) % 5) * 128, 128)
+
+    def to_core(yl, n):
+        return copy(acc.at[yl, :, lanes(n)], sum_in.at[:, lanes(n)], sem(s_c1, n), sem(r_c1, n), core)
+
+    def to_mate(m):
+        return copy(chip_out.at[:, along_y(m)], chip_in.at[:, along_y(m)], sem(s_m, m), sem(r_m, m), mate)
+
+    def back_to_core(yl, n):
+        piece = rot.at[yl, :, lanes(n)]
+        return copy(piece, piece, sem(s_c2, n), sem(r_c2, n), core)
+
+    def chip_sum(yl, n):
+        ln = lanes(n)
+        landed(sum_in.at[:, ln], sem(r_c1, n))
+        total = acc[yl, :, ln] + sum_in[:, ln]
+        acc[yl, :, ln] = total
+        chip_out[:, ln] = total.astype(BF16)
+        for m in COPIES[n]:
+            to_mate(m).start()
+
+    def finish(yl, n):
+        ln = lanes(n)
+        for m in COPIES[n]:
+            landed(chip_in.at[:, along_y(m)], sem(r_m, m))
+        rot[yl, :, ln] = (acc[yl, :, ln] + chip_in[:, ln].astype(F32)).astype(BF16)
+        back_to_core(yl, n).start()
+
+    for n in range(3):
+        product(early, n)
+
+        @pl.when(sums_late)
+        def _():
+            to_core(early, n).start()
 
     alphas(10, 12)
     side_beta(3)
-    landed(g_full.at[x_prev], sem(gr_x))
-    send(g_full.at[x_prev, half_a], g_full.at[x_prev, half_a], sem(gs_x, 2), sem(gr_x, 2), right)
-    landed(g_full.at[x_next], sem(gr_x, 1))
-    send(g_full.at[x_next, half_b], g_full.at[x_next, half_b], sem(gs_x, 3), sem(gr_x, 3), left)
+    for i, o in enumerate(OTHER):
+        q = on_x(o)
+        landed(g_full.at[q, low], sem(gr_x, q))
+        send(g_full.at[q, low], g_full.at[q, low], sem(gs_v, i), sem(gr_v, q), device(x, y + 2, z, c))
 
     @pl.when(sums_early)
     def _():
-        chip_sum(early)
+        for n in range(3):
+            chip_sum(early, n)
 
     alphas(12, 16)
     far_beta(2)
     far_beta(3)
-    product(late)
-
-    @pl.when(sums_early)
-    def _():
-        to_core(late).start()
-
-    landed(g_full.at[x_far, half_a], sem(gr_x, 2))
-    landed(g_full.at[x_far, half_b], sem(gr_x, 3))
+    def late_product(n):
+        product(late, n)
+
+        @pl.when(sums_early)
+        def _():
+            to_core(late, n).start()
+
+    def late_sum(n):
+        @pl.when(sums_late)
+        def _():
+            chip_sum(late, n)
+            finish(late, n)
+
+    late_product(0)
+    late_product(1)
+    late_sum(0)
+    late_product(2)
+    late_sum(1)
+    late_sum(2)
+
+    for o in OTHER:
+        landed(g_full.at[on_x(o), high], sem(gr_v, on_x(o)))
 
     def transpose(q, carry):
         g_train_t[q] = g_full[q, 0:TOK_DP, :].astype(F32).T.astype(BF16)
@@ -447,19 +497,24 @@
 
     lax.fori_loop(0, 4, transpose, 0)
 
-    @pl.when(jnp.logical_not(sums_early))
-    def _():
-        chip_sum(late)
-        finish(late)
-
-    @pl.when(sums_early)
-    def _():
-        finish(early)
-        landed(rot.at[late], sem(r_c2))
-
-    @pl.when(jnp.logical_not(sums_early))
-    def _():
-        landed(rot.at[early], sem(r_c2))
+    def finish_early(n):
+        @pl.when(sums_early)
+        def _():
+            finish(early, n)
+
+    def await_early(n):
+        @pl.when(sums_late)
+        def _():
+            landed(rot.at[early, :, lanes(n)], sem(r_c2, n))
+
+    def await_late(n):
+        @pl.when(sums_early)
+        def _():
+            landed(rot.at[late, :, lanes(n)], sem(r_c2, n))
+
+    finish_early(0)
+    await_early(0)
+    await_late(0)
 
     query_rot = jnp.concatenate([rot[0, :, TRAIN:], rot[1, :, TRAIN:]], axis=1).astype(F32)
     query_grad = jnp.concatenate([g_full[q, TOK_DP:, :] for q in range(4)], axis=0)
@@ -467,26 +522,39 @@
         masked = jnp.where(pid[...] == p, query_rot, 0.0).astype(BF16)
         precond[p] = (jnp.dot(masked, query_grad, preferred_element_type=F32) * recip[...]).astype(BF16)
 
-    def token_scores(q, carry):
-        lanes = pl.ds(pl.multiple_of((q % 2) * TOK_DP, 128), TOK_DP)
-        train = rot[q // 2, :, lanes].astype(F32)
+    def token_scores(yl, cc):
+        train = rot[yl, :, lanes(1 + cc)].astype(F32)
         rows = []
         for p in range(PAIRS):
-            projected = jnp.dot(precond[p], g_train_t[q], preferred_element_type=F32)
+            projected = jnp.dot(precond[p], g_train_t[2 * yl + cc], preferred_element_type=F32)
             rows.append(jnp.sum(projected * train, axis=0, keepdims=True))
         rows.append(jnp.zeros((8 - PAIRS, TOK_DP), F32))
-        tok[q % 2, q // 2] = jnp.concatenate(rows, axis=0)
-        return carry
-
-    lax.fori_loop(0, 4, token_scores, 0)
-
-    ts_c, tr_c, ts_y, tr_y = (names.take() for _ in range(4))
-    send(tok.at[1 - c], tok_in, sem(ts_c), sem(tr_c), core)
-    landed(tok_in, sem(tr_c))
-    tok_y[...] = tok[c] + tok_in[...]
-    send(tok_y.at[1 - k], tok_yin, sem(ts_y), sem(tr_y), mate)
-    landed(tok_yin, sem(tr_y))
-    scores = tok_y[k] + tok_yin[...]
+        tok[cc, yl] = jnp.concatenate(rows, axis=0)
+
+    finish_early(1)
+    await_late(1)
+    token_scores(late, 0)
+    finish_early(2)
+    await_late(2)
+    token_scores(late, 1)
+    await_early(1)
+    token_scores(early, 0)
+    await_early(2)
+    token_scores(early, 1)
+
+    ts, tr = names.take(7), names.take(8)
+    own_slot = 2 * y + c
+    tok_in[own_slot] = tok[c, k]
+    to = [(o, cc) for o in (0, 1, 3, 2) for cc in (0, 1)][1:]
+    for i, (o, cc) in enumerate(to):
+        src = tok.at[(c + cc) % 2, (k + o) % 2]
+        send(src, tok_in.at[own_slot], sem(ts, i), sem(tr, own_slot), device(x, y + o, z, (c + cc) % 2))
+    for o, cc in to:
+        at = 2 * on_y(o) + (c + cc) % 2
+        landed(tok_in.at[at], sem(tr, at))
+    scores = tok_in[0]
+    for i in range(1, 8):
+        scores = scores + tok_in[i]
 
     lane = lax.broadcasted_iota(jnp.int32, (8, TOK_DP), 1)
     column = lax.broadcasted_iota(jnp.int32, (8, 128), 1)
@@ -509,11 +577,7 @@
         for o in OTHER:
             landed(buf.at[(at + o) % 4], sem(r_red, (at + o) % 4))
         result = (buf[0] + buf[1]) + (buf[2] + buf[3])
-    s_red, r_red = names.take(), names.take()
-    red_y[y // 2] = result
-    send(red_y.at[y // 2], red_y.at[y // 2], sem(s_red), sem(r_red), device(x, y + 2, z, c))
-    landed(red_y.at[1 - y // 2], sem(r_red))
-    out[...] = (red_y[0] + red_y[1]) * SCALE
+    out[...] = result * SCALE
 
     for cp in sent:
         cp.wait_send()
@@ -538,14 +602,17 @@
     def _():
         for i in range(3):
             z_beta(i, True).wait_send()
-            x_alpha(i, True).wait_send()
+            for h in range(PARTS):
+                x_alpha(i, True, h).wait_send()
         for i in range(4):
-            y_alpha_own(i, x).wait_send()
+            for h in range(PARTS):
+                y_alpha_own(i, x, h).wait_send()
 
     @pl.when(is_other)
     def _():
         for i in range(4):
-            y_alpha_other(i, x, 3).wait_send()
+            for h in range(PARTS):
+                y_alpha_other(i, x, 3, h).wait_send()
 
     def drain_x(n, carry):
         x_beta(n, x, y, 1).wait_send()
@@ -556,14 +623,17 @@
     @pl.when(pi != 3)
     def _():
         def drain_z(t, carry):
-            z_alpha(t, x, y).wait_send()
+            for h in range(PARTS):
+                z_alpha(t, x, y, h).wait_send()
             return carry
 
         lax.fori_loop(0, 16, drain_z, 0)
 
-    to_core(0).wait_send()
-    to_mate().wait_send()
-    back_to_core(0).wait_send()
+    for n in range(3):
+        to_core(0, n).wait_send()
+        back_to_core(0, n).wait_send()
+    for m in range(5):
+        to_mate(m).wait_send()
 
     assert names.used <= N_SEMS
 
@@ -605,12 +675,9 @@
             v((2, COLS, LANES)),
             v((PAIRS, COLS, QUART)),
             v((2, 2, 8, TOK_DP), F32),
-            v((2, 8, TOK_DP), F32),
-            v((2, 8, TOK_DP), F32),
-            v((8, TOK_DP), F32),
+            v((8, 8, TOK_DP), F32),
             v((4, 8, 128), F32),
             v((4, 8, 128), F32),
-            v((2, 8, 128), F32),
             pltpu.SemaphoreType.DMA((N_SEMS,)),
         ],
         compiler_params=pltpu.CompilerParams(

time: 184 us -> 163 us (0.89)
  Pallas kernels: 182 us -> 162 us
    pallas_call x1, Pallas kernels: 182 us -> 162 us  [fused(): pl.pallas_call(kernel, out_shape=jax.ShapeDtypeStruct((8, 128), F32), in_...]
where the time goes in v3:
time: 163 us
  Pallas kernels  162 us (99%)
    pallas_call x1, Pallas kernels, fused(): pl.pallas_call(kernel, out_shape=jax.ShapeDtypeStruct((8, 128), F32), in_...  162 us

profile of v3, /device:TPU:0, one launch (start us, length us, event | category | flops | bytes accessed | tf_op | source)
XLA Modules:
  0.0 163.2 jit_solution(16127105493541436371)
XLA Ops:
  0.0 162.0 %influence.1 = f32[8,128]{1,0:T(8,128)} custom-call(bf16[592,256]{1,0:T(8,128)(2,1)} %bitcast.7, bf16[64,592]{1,0:T(8,128)(2,1)} %query.1, bf16[112,256]{1,0:T(8,128)(2,1)} %bitcast.8, bf16[64,112]{1,0:T(8,128)(2,1)} %query_g.1, s32[1,256]{1,0:T(1,128)} %bitcast.9, s32[1,4]{1,0:T(1,128)} %lengths.1, bf16[592,4736]{1,0:T(8,128)(2,1)} %bitcast.5, ...), custom_call_target="tpu_custom_call" | custom-call | flops 12609126400 | bytes 20971520 | tf_op jit(solution)/shard_map/influence/pallas_call | solution.py:648
  162.0 1.3 slice.3

commit v4 on v3

--- a/solution.py
+++ b/solution.py
@@ -55,14 +55,14 @@
         return self.used - n
 
 
-N_SEMS = 256
+N_SEMS = 320
 
 
 def kernel(
     train_t, query, train_g_t, query_g, pid, lengths, w_hbm, eig_hbm, ob_hbm, out,
     units, other, w, acc, query_t, query_in, eig, recip,
     og_tok, og_feat, ob, g_sum, g_part, g_rz, g_yb, g_ry, g_full, g_train_t,
-    sum_in, chip_out, chip_in, rot, precond, tok, tok_in, red_x, red_z,
+    sum_in, chip_out, chip_in, rot, precond, tok, tok_in, red,
     sems,
 ):
     x, y, z, c = place()
@@ -104,6 +104,7 @@
     partners += [device(x, y, z + o, c) for o in OTHER]
     core = device(x, y, z, 1 - c)
     partners += [core] + [device(x, y + o, z, 1 - c) for o in OTHER]
+    partners += [device(x + ox, y, z + oz, c) for ox in OTHER for oz in OTHER]
     mate = device(x, y + 1 - 2 * k, z, c)
 
     def landed(dst, recv):
@@ -131,11 +132,6 @@
     eig_copy = pltpu.make_async_copy(eig_hbm.at[:, quarter], eig, sem(s_eig))
     eig_copy.start()
 
-    barrier = pltpu.get_barrier_semaphore()
-    for p in partners:
-        pl.semaphore_signal(barrier, inc=1, device_id=p, device_id_type=MESH)
-    pl.semaphore_wait(barrier, len(partners))
-
     turned = query[...].astype(F32).T.astype(BF16)
     nothing = jnp.zeros_like(turned)
     query_t[...] = jnp.concatenate(
@@ -143,6 +139,11 @@
     )
     og_tok[d, 0:TOK_DP, :] = train_g_t[...].astype(F32).T.astype(BF16)
     og_tok[d, TOK_DP:, :] = query_g[...]
+
+    barrier = pltpu.get_barrier_semaphore()
+    for p in partners:
+        pl.semaphore_signal(barrier, inc=1, device_id=p, device_id_type=MESH)
+    pl.semaphore_wait(barrier, len(partners))
 
     gs_c, gr_c = names.take(), names.take()
     send(og_tok.at[d], og_tok.at[d], sem(gs_c), sem(gr_c), core)
@@ -317,7 +318,6 @@
     own_beta(1)
     alphas(2, 4)
 
-    side_beta(0)
     for o in OTHER:
         xs = (x + o) % 4
         landed(og_feat.at[xs], sem(gr_f, xs))
@@ -338,6 +338,7 @@
     for i, o in enumerate(OTHER):
         send(g_part.at[chunk(z + o)], g_rz.at[z], sem(gs_z, i), sem(gr_z, z), device(x, y, z + o, c))
 
+    side_beta(0)
     eig_copy.wait()
     recip[...] = 1.0 / (eig[...].astype(F32) + DAMPING)
 
@@ -359,8 +360,6 @@
                 y_alpha_other(i + 1, on_x(dx), 3, h).start()
 
     alphas(4, 5)
-    side_beta(1)
-    alphas(5, 6)
     total = g_sum[chunk(z), :]
     for o in OTHER:
         zz = (z + o) % 4
@@ -371,7 +370,8 @@
     gs_h, gr_h = names.take(), names.take()
     send(g_yb, g_ry, sem(gs_h), sem(gr_h), device(x, y + 2, z, c))
 
-    alphas(6, 8)
+    side_beta(1)
+    alphas(5, 6)
     landed(g_ry, sem(gr_h))
     g_full[x, chunk(z), :] = (g_sum[chunk(z), :] + g_ry[...].astype(F32)).astype(BF16)
     gs_g, gr_g = names.take(3), names.take(4)
@@ -379,6 +379,7 @@
         piece = g_full.at[x, chunk(z)]
         send(piece, piece, sem(gs_g, i), sem(gr_g, z), device(x, y, z + o, c))
 
+    alphas(6, 8)
     side_beta(2)
     alphas(8, 9)
     for o in OTHER:
@@ -566,17 +567,18 @@
         result = jnp.where(column == n, part, result)
         start = end
 
-    for buf, at, target in (
-        (red_x, x, lambda o: device(x + o, y, z, c)),
-        (red_z, z, lambda o: device(x, y, z + o, c)),
-    ):
-        s_red, r_red = names.take(3), names.take(4)
-        buf[at] = result
-        for i, o in enumerate(OTHER):
-            send(buf.at[at], buf.at[at], sem(s_red, i), sem(r_red, at), target(o))
-        for o in OTHER:
-            landed(buf.at[(at + o) % 4], sem(r_red, (at + o) % 4))
-        result = (buf[0] + buf[1]) + (buf[2] + buf[3])
+    s_red, r_red = names.take(15), names.take(16)
+    at = 4 * z + x
+    red[at] = result
+    away = [(ox, oz) for oz in range(4) for ox in range(4)][1:]
+    for i, (ox, oz) in enumerate(away):
+        send(red.at[at], red.at[at], sem(s_red, i), sem(r_red, at), device(x + ox, y, z + oz, c))
+    for ox, oz in away:
+        there = 4 * ((z + oz) % 4) + (x + ox) % 4
+        landed(red.at[there], sem(r_red, there))
+    result = red[0]
+    for i in range(1, 16):
+        result = result + red[i]
     out[...] = result * SCALE
 
     for cp in sent:
@@ -676,8 +678,7 @@
             v((PAIRS, COLS, QUART)),
             v((2, 2, 8, TOK_DP), F32),
             v((8, 8, TOK_DP), F32),
-            v((4, 8, 128), F32),
-            v((4, 8, 128), F32),
+            v((16, 8, 128), F32),
             pltpu.SemaphoreType.DMA((N_SEMS,)),
         ],
         compiler_params=pltpu.CompilerParams(

time: 163 us -> 163 us (level)
  no operation moved by 1% of the time
where the time goes in v4:
time: 163 us
  Pallas kernels  161 us (99%)
    pallas_call x1, Pallas kernels, fused(): pl.pallas_call(kernel, out_shape=jax.ShapeDtypeStruct((8, 128), F32), in_...  161 us

profile of v4, /device:TPU:0, one launch (start us, length us, event | category | flops | bytes accessed | tf_op | source)
XLA Modules:
  0.0 162.5 jit_solution(18407759393798142709)
XLA Ops:
  0.0 161.2 %influence.1 = f32[8,128]{1,0:T(8,128)} custom-call(bf16[592,256]{1,0:T(8,128)(2,1)} %bitcast.7, bf16[64,592]{1,0:T(8,128)(2,1)} %query.1, bf16[112,256]{1,0:T(8,128)(2,1)} %bitcast.8, bf16[64,112]{1,0:T(8,128)(2,1)} %query_g.1, s32[1,256]{1,0:T(1,128)} %bitcast.9, s32[1,4]{1,0:T(1,128)} %lengths.1, bf16[592,4736]{1,0:T(8,128)(2,1)} %bitcast.5, ...), custom_call_target="tpu_custom_call" | custom-call | flops 12609126400 | bytes 20971520 | tf_op jit(solution)/shard_map/influence/pallas_call | solution.py:650
  161.3 1.3 slice.3

commit v5 on v4

--- a/solution.py
+++ b/solution.py
@@ -28,9 +28,11 @@
 MESH = pl.DeviceIdType.MESH
 F32, BF16 = jnp.float32, jnp.bfloat16
 
-RB = 368
-PARTS = 2
+RB = 352
+PARTS = 3
 RA = (COLS - RB) // PARTS
+PB = 2
+RP = RB // PB
 OTHER = (1, 3, 2)
 CHUNKS = ((TRAIN, LANES - TRAIN), (0, TOK_DP), (TOK_DP, TOK_DP))
 COPIES = ((0,), (1, 2), (3, 4))
@@ -55,7 +57,7 @@
         return self.used - n
 
 
-N_SEMS = 320
+N_SEMS = 420
 
 
 def kernel(
@@ -85,8 +87,14 @@
         rows = pl.ds(pl.multiple_of(COLS * (4 * (ys // 2) + xs) + low, 16), count)
         return units.at[ys % 2, rows] if lanes is None else units.at[ys % 2, rows, lanes]
 
-    def beta(xs, ys):
-        return unit(xs, ys, 0, RB)
+    def beta(xs, ys, g):
+        return unit(xs, ys, g * RP, RP)
+
+    def other_beta(g):
+        return other.at[x, pl.ds(g * RP, RP)]
+
+    def got_beta(xs, ys, g):
+        return sem(r_b, PB * slot(xs, ys) + g)
 
     def alpha(xs, ys, h):
         return unit(xs, ys, RB + h * RA, RA)
@@ -120,8 +128,8 @@
     dummy = names.take()
     s_w, s_eig, s_ob, s_own = names.take(), names.take(), names.take(), names.take()
     s_step, r_step = names.take(2), names.take(2)
-    r_b, r_a, r_ob, r_oa = names.take(16), names.take(16 * PARTS), names.take(), names.take(4 * PARTS)
-    s_zb, s_yb, s_xb = names.take(3), names.take(3), names.take(12)
+    r_b, r_a, r_ob, r_oa = names.take(16 * PB), names.take(16 * PARTS), names.take(PB), names.take(4 * PARTS)
+    s_zb, s_yb, s_xb = names.take(3 * PB), names.take(3 * PB), names.take(12 * PB)
     s_xa, s_ya, s_ya2, s_za = (names.take(n * PARTS) for n in (3, 4, 4, 16))
 
     w_copy = pltpu.make_async_copy(w_hbm, w, sem(s_w))
@@ -168,9 +176,10 @@
     def _():
         to_query.start()
 
-    def z_beta(i, own):
-        piece = beta(x, y) if own else other.at[x, pl.ds(0, RB)]
-        return copy(piece, piece, sem(s_zb, i), sem(r_b, slot(x, y)) if own else sem(r_ob), device(x, y, z + OTHER[i], c))
+    def z_beta(i, own, g):
+        piece = beta(x, y, g) if own else other_beta(g)
+        got = got_beta(x, y, g) if own else sem(r_ob, g)
+        return copy(piece, piece, sem(s_zb, PB * i + g), got, device(x, y, z + OTHER[i], c))
 
     def got_alpha(xs, ys, h):
         return sem(r_a, PARTS * slot(xs, ys) + h)
@@ -192,17 +201,16 @@
         sent_by = sem(s_ya if step == 1 else s_ya2, PARTS * i + h)
         return copy(other_alpha(xs, h), alpha(xs, y, h), sent_by, got_alpha(xs, y, h), device(x, y + step, z, c))
 
-    def y_beta_own():
-        piece = beta(x, y)
-        return copy(piece, piece, sem(s_yb, 2), sem(r_b, slot(x, y)), device(x, y + 2, z, c))
-
-    def y_beta_other(i):
-        src = other.at[x, pl.ds(0, RB)]
-        return copy(src, beta(x, y), sem(s_yb, i), sem(r_b, slot(x, y)), device(x, y + OTHER[i], z, c))
-
-    def x_beta(n, xs, ys, step):
-        piece = beta(xs, ys)
-        return copy(piece, piece, sem(s_xb, n), sem(r_b, slot(xs, ys)), device(x + step, y, z, c))
+    def y_beta_own(g):
+        piece = beta(x, y, g)
+        return copy(piece, piece, sem(s_yb, 2 * PB + g), got_beta(x, y, g), device(x, y + 2, z, c))
+
+    def y_beta_other(i, g):
+        return copy(other_beta(g), beta(x, y, g), sem(s_yb, PB * i + g), got_beta(x, y, g), device(x, y + OTHER[i], z, c))
+
+    def x_beta(n, xs, ys, step, g):
+        piece = beta(xs, ys, g)
+        return copy(piece, piece, sem(s_xb, PB * n + g), got_beta(xs, ys, g), device(x + step, y, z, c))
 
     def gather_step(dst_mine, dst_theirs, dst_tail):
         own = pltpu.make_async_copy(train_t, dst_mine, sem(s_own))
@@ -215,16 +223,20 @@
     @pl.when(is_own)
     def _():
         gather_step(unit(x, y, 0, COLS, mine), unit(x, y, 0, COLS, theirs), unit(x, y, 0, COLS, tail))
+        for g in range(PB):
+            for i in range(3):
+                z_beta(i, True, g).start()
         for i in range(3):
-            z_beta(i, True).start()
             for h in range(PARTS):
                 x_alpha(i, True, h).start()
 
     @pl.when(is_other)
     def _():
         gather_step(other.at[x, :, mine], other.at[x, :, theirs], other.at[x, :, tail])
+        for g in range(PB):
+            for i in range(3):
+                z_beta(i, False, g).start()
         for i in range(3):
-            z_beta(i, False).start()
             for h in range(PARTS):
                 x_alpha(i, False, h).start()
         for h in range(PARTS):
@@ -274,37 +286,43 @@
 
     def own_beta(i):
         ys = on_y(BETA[i])
-        if i == 0:
-
-            @pl.when(jnp.logical_not(is_own))
-            def _():
-                landed(beta(x, ys), sem(r_b, slot(x, ys)))
-        else:
-            landed(beta(x, ys), sem(r_b, slot(x, ys)))
-        x_beta(2 * i, x, ys, 1).start()
-        x_beta(2 * i + 1, x, ys, 3).start()
+        for g in range(PB):
+            if i == 0:
+
+                @pl.when(jnp.logical_not(is_own))
+                def _():
+                    landed(beta(x, ys, g), got_beta(x, ys, g))
+            else:
+                landed(beta(x, ys, g), got_beta(x, ys, g))
+            x_beta(2 * i, x, ys, 1, g).start()
+            x_beta(2 * i + 1, x, ys, 3, g).start()
+            if i == 0:
+                y_beta_own(g).start()
 
     def side_beta(i):
         ys = on_y(BETA[i])
         order = ((3, 1), (1, 3))[i % 2]
         for n, dx in enumerate(order):
-            landed(beta(on_x(dx), ys), sem(r_b, slot(on_x(dx), ys)))
-            if n == 0:
-                x_beta(8 + i, on_x(dx), ys, 4 - dx).start()
+            for g in range(PB):
+                landed(beta(on_x(dx), ys, g), got_beta(on_x(dx), ys, g))
+                if n == 0:
+                    x_beta(8 + i, on_x(dx), ys, 4 - dx, g).start()
 
     def far_beta(i):
         ys = on_y(BETA[i])
-        landed(beta(on_x(2), ys), sem(r_b, slot(on_x(2), ys)))
+        for g in range(PB):
+            landed(beta(on_x(2), ys, g), got_beta(on_x(2), ys, g))
 
     own_beta(0)
-    y_beta_own().start()
-
-    @pl.when(jnp.logical_not(is_other))
-    def _():
-        landed(other.at[x, pl.ds(0, RB)], sem(r_ob))
-
-    y_beta_other(0).start()
-    y_beta_other(1).start()
+
+    for g in range(PB):
+
+        @pl.when(jnp.logical_not(is_other))
+        def _():
+            landed(other_beta(g), sem(r_ob, g))
+
+        y_beta_other(0, g).start()
+        y_beta_other(1, g).start()
     alphas(0, 2)
 
     landed(og_tok.at[2 * (1 - k)], sem(gr_y))
@@ -596,14 +614,16 @@
     def _():
         to_query.wait_send()
 
-    for i in range(2):
-        y_beta_other(i).wait_send()
-    y_beta_own().wait_send()
+    for g in range(PB):
+        for i in range(2):
+            y_beta_other(i, g).wait_send()
+        y_beta_own(g).wait_send()
 
     @pl.when(is_own | is_other)
     def _():
         for i in range(3):
-            z_beta(i, True).wait_send()
+            for g in range(PB):
+                z_beta(i, True, g).wait_send()
             for h in range(PARTS):
                 x_alpha(i, True, h).wait_send()
         for i in range(4):
@@ -617,7 +637,8 @@
                 y_alpha_other(i, x, 3, h).wait_send()
 
     def drain_x(n, carry):
-        x_beta(n, x, y, 1).wait_send()
+        for g in range(PB):
+            x_beta(n, x, y, 1, g).wait_send()
         return carry
 
     lax.fori_loop(0, 12, drain_x, 0)

time: 163 us -> 162 us (level)
  no operation moved by 1% of the time
where the time goes in v5:
time: 162 us; the launch traced here: 161 us
  Pallas kernels  160 us (99%)
    pallas_call x1, Pallas kernels, fused(): pl.pallas_call(kernel, out_shape=jax.ShapeDtypeStruct((8, 128), F32), in_...  160 us

profile of v5, /device:TPU:0, one launch (start us, length us, event | category | flops | bytes accessed | tf_op | source)
XLA Modules:
  0.0 161.3 jit_solution(7275947014058689744)
XLA Ops:
  0.0 160.0 %influence.1 = f32[8,128]{1,0:T(8,128)} custom-call(bf16[592,256]{1,0:T(8,128)(2,1)} %bitcast.7, bf16[64,592]{1,0:T(8,128)(2,1)} %query.1, bf16[112,256]{1,0:T(8,128)(2,1)} %bitcast.8, bf16[64,112]{1,0:T(8,128)(2,1)} %query_g.1, s32[1,256]{1,0:T(1,128)} %bitcast.9, s32[1,4]{1,0:T(1,128)} %lengths.1, bf16[592,4736]{1,0:T(8,128)(2,1)} %bitcast.5, ...), custom_call_target="tpu_custom_call" | custom-call | flops 12609126400 | bytes 20971520 | tf_op jit(solution)/shard_map/influence/pallas_call | solution.py:671
  160.0 1.3 slice.3

commit v6 on v5

--- a/solution.py
+++ b/solution.py
@@ -156,6 +156,11 @@
     gs_c, gr_c = names.take(), names.take()
     send(og_tok.at[d], og_tok.at[d], sem(gs_c), sem(gr_c), core)
 
+    ob_copy.wait()
+    gs_ob, gr_ob = names.take(3), names.take(4)
+    for i, o in enumerate(OTHER):
+        send(ob.at[x], ob.at[x], sem(gs_ob, i), sem(gr_ob, x), device(x + o, y, z, c))
+
     mine = pl.ds(pl.multiple_of(c * TOK_DP, 128), TOK_DP)
     theirs = pl.ds(pl.multiple_of((1 - c) * TOK_DP, 128), TOK_DP)
     tail = pl.ds(TRAIN, LANES - TRAIN)
@@ -252,11 +257,6 @@
     landed(og_tok.at[2 * k + 1 - c], sem(gr_c))
     send(og_tok.at[2 * k], og_tok.at[2 * k], sem(gs_y), sem(gr_y), mate)
     send(og_tok.at[2 * k + 1], og_tok.at[2 * k + 1], sem(gs_y, 1), sem(gr_y, 1), mate)
-    ob_copy.wait()
-    gs_ob, gr_ob = names.take(3), names.take(4)
-    for i, o in enumerate(OTHER):
-        send(ob.at[x], ob.at[x], sem(gs_ob, i), sem(gr_ob, x), device(x + o, y, z, c))
-
     ALPHA = [(0, 0), (1, 0), (3, 0), (2, 0), (0, 2), (0, 1), (0, 3), (1, 2), (3, 2), (2, 2)]
     ALPHA += [(1, 1), (1, 3), (3, 1), (3, 3), (2, 1), (2, 3)]
     BETA = (0, 2, 1, 3)
@@ -336,6 +336,21 @@
     own_beta(1)
     alphas(2, 4)
 
+    @pl.when(is_own)
+    def _():
+        for i, dx in enumerate(OTHER):
+            for h in range(PARTS):
+                y_alpha_own(i + 1, on_x(dx), h).start()
+
+    @pl.when(is_other)
+    def _():
+        for i, dx in enumerate(OTHER):
+            for h in range(PARTS):
+                landed(other_alpha(on_x(dx), h), sem(r_oa, PARTS * on_x(dx) + h))
+                y_alpha_other(i + 1, on_x(dx), 1, h).start()
+                y_alpha_other(i + 1, on_x(dx), 3, h).start()
+
+
     for o in OTHER:
         xs = (x + o) % 4
         landed(og_feat.at[xs], sem(gr_f, xs))
@@ -362,20 +377,6 @@
 
     own_beta(2)
     own_beta(3)
-
-    @pl.when(is_own)
-    def _():
-        for i, dx in enumerate(OTHER):
-            for h in range(PARTS):
-                y_alpha_own(i + 1, on_x(dx), h).start()
-
-    @pl.when(is_other)
-    def _():
-        for i, dx in enumerate(OTHER):
-            for h in range(PARTS):
-                landed(other_alpha(on_x(dx), h), sem(r_oa, PARTS * on_x(dx) + h))
-                y_alpha_other(i + 1, on_x(dx), 1, h).start()
-                y_alpha_other(i + 1, on_x(dx), 3, h).start()
 
     alphas(4, 5)
     total = g_sum[chunk(z), :]

time: 162 us -> 160 us (0.988)
  Pallas kernels: 160 us -> 158 us
    pallas_call x1, Pallas kernels: 160 us -> 158 us  [fused(): pl.pallas_call(kernel, out_shape=jax.ShapeDtypeStruct((8, 128), F32), in_...]
where the time goes in v6:
time: 160 us
  Pallas kernels  158 us (99%)
    pallas_call x1, Pallas kernels, fused(): pl.pallas_call(kernel, out_shape=jax.ShapeDtypeStruct((8, 128), F32), in_...  158 us

profile of v6, /device:TPU:0, one launch (start us, length us, event | category | flops | bytes accessed | tf_op | source)
XLA Modules:
  0.0 159.6 jit_solution(11789725995471580854)
XLA Ops:
  0.0 158.3 %influence.1 = f32[8,128]{1,0:T(8,128)} custom-call(bf16[592,256]{1,0:T(8,128)(2,1)} %bitcast.7, bf16[64,592]{1,0:T(8,128)(2,1)} %query.1, bf16[112,256]{1,0:T(8,128)(2,1)} %bitcast.8, bf16[64,112]{1,0:T(8,128)(2,1)} %query_g.1, s32[1,256]{1,0:T(1,128)} %bitcast.9, s32[1,4]{1,0:T(1,128)} %lengths.1, bf16[592,4736]{1,0:T(8,128)(2,1)} %bitcast.5, ...), custom_call_target="tpu_custom_call" | custom-call | flops 12609126400 | bytes 20971520 | tf_op jit(solution)/shard_map/influence/pallas_call | solution.py:672
  158.3 1.3 slice.3
